TPU v7x, 256 devices: a whole 4x4x8 slice. The times are simulated.
256 devices in a mesh: grp: 16 (over z, y_hi), ep: 16 (over y_lo, x, core).
Axes of the slice: x: 4, y: 4 (y_hi: 2, y_lo: 2; y = y_hi * 2 + y_lo), z: 8, core: 2. Of those that a mesh axis runs over, the one named last changes fastest.
Arguments:
- tokens: bfloat16 [49152, 4096], P(('grp', 'ep')), may hold values from -6 to 6
- expert_ids: int32 [49152, 8], P(('grp', 'ep')), may hold values from 0 to 127, all different within a row; in each aligned block of 192 rows (0 to 191, 192 to 383, ...) at most 24 rows name the same one
- gate_probs: float32 [49152, 8], P(('grp', 'ep')), may hold values from 0.02 to 0.25
- placement: int32 [16, 4], P('grp'), may hold values from 0 to 1
- gate_weight: bfloat16 [16, 4096, 3072], P('grp', None, 'ep'), may hold values from -0.09375 to 0.09375
- up_weight: bfloat16 [16, 4096, 3072], P('grp', None, 'ep'), may hold values from -0.09375 to 0.09375
- down_weight: bfloat16 [16, 3072, 4096], P('grp', 'ep'), may hold values from -0.21875 to 0.21875
- out_grad: bfloat16 [49152, 4096], P(('grp', 'ep')), may hold values from -6 to 6
- moment_first: float32 [2, 3072, 4096], P(None, 'ep', 'grp'), may hold values from -2 to 2
- moment_second: float32 [2, 3072, 4096], P(None, 'ep', 'grp'), may hold values from 0.01 to 1
Outputs:
- token_grad: bfloat16 [49152, 4096], P(('grp', 'ep'))
- step_dir: bfloat16 [16, 3072, 4096], P('grp', 'ep')
- new_first: float32 [2, 3072, 4096], P(None, 'ep', 'grp')
- new_second: float32 [2, 3072, 4096], P(None, 'ep', 'grp')
Inputs may be any that keep to these rules, and one draw needn't show every extreme that they name: `expert_ids`: each row names 8 different experts. In the rows of one device no expert is named more than 24 times, a bound that some block reaches. Group g holds expert placement[g, s] * 4 + s in its slot s.
All inputs are finite; a program needn't handle non-finite values.
Results may differ from a plain program's by a relative error of at most 0.015.
Values may be sent and summed in bfloat16 or wider, within the bound.
A program may use at most 128 MiB of HBM per device.

v0:
```python
import math

import jax
import jax.numpy as jnp
from jax import lax
from jax.sharding import PartitionSpec as P

QUARTERS = 4
CANDS = 2
CAP = 24


beta_one = 0.9
beta_two = 0.999
adam_eps = 1e-08
first_fix = 1.0 - math.exp(1000.0 * math.log(0.9))
second_fix = 1.0 - math.exp(1000.0 * math.log(0.999))


def moments(gradient, first_moment, second):
    new_first = beta_one * first_moment + (1.0 - beta_one) * gradient
    new_second = beta_two * second + (1.0 - beta_two) * gradient * gradient
    return (new_first, new_second)


def direction(new_first, new_second):
    return new_first / first_fix / (jnp.sqrt(new_second / second_fix) + adam_eps)


def body(
    tokens,
    expert_ids,
    gate_probs,
    placement,
    gate_weight,
    up_weight,
    down_weight,
    out_grad,
    moment_first,
    moment_second,
):
    num_ep = lax.axis_size("ep")
    slot_count = num_ep // QUARTERS
    tok_count = tokens.shape[0]
    width = tokens.shape[1]
    held_ids = placement[0] * slot_count + jnp.arange(slot_count, dtype=jnp.int32)
    matches = expert_ids[:, :, None] == held_ids[None, None, :]
    hit_rows = jnp.any(matches, axis=1)
    coeffs = jnp.sum(jnp.where(matches, gate_probs[:, :, None], jnp.float32(0.0)), axis=1)
    ranking = jnp.cumsum(hit_rows.astype(jnp.int32), axis=0) - 1
    select_mask = hit_rows.T[:, None, :] & (
        ranking.T[:, None, :] == jnp.arange(CAP, dtype=jnp.int32)[None, :, None]
    )
    select_flat = select_mask.reshape(slot_count * CAP, tok_count).astype(jnp.bfloat16)
    send_tokens = jnp.dot(select_flat, tokens, preferred_element_type=jnp.float32).astype(
        jnp.bfloat16
    )
    send_grads = jnp.dot(select_flat, out_grad, preferred_element_type=jnp.float32).astype(
        jnp.bfloat16
    )
    send_coeffs = jnp.sum(select_mask.astype(jnp.float32) * coeffs.T[:, None, :], axis=2)

    def spread(source):
        shaped = source.reshape(slot_count, 1, CAP, width)
        return jnp.broadcast_to(shaped, (slot_count, QUARTERS, CAP, width)).reshape(
            num_ep, CAP, width
        )

    coeff_spread = jnp.broadcast_to(send_coeffs[:, None, :], (slot_count, QUARTERS, CAP)).reshape(
        num_ep, CAP
    )
    w_gate = gate_weight[0]
    w_up = up_weight[0]
    w_down = down_weight[0]
    recv_tokens, recv_grads, recv_coeffs = (
        lax.all_to_all(spread(send_tokens), "ep", split_axis=0, concat_axis=0, tiled=True),
        lax.all_to_all(spread(send_grads), "ep", split_axis=0, concat_axis=0, tiled=True),
        lax.all_to_all(
            coeff_spread.astype(jnp.bfloat16), "ep", split_axis=0, concat_axis=0, tiled=True
        ).astype(coeff_spread.dtype),
    )
    in_rows = recv_tokens.reshape(num_ep * CAP, width)
    pre_gate = jnp.dot(in_rows, w_gate, preferred_element_type=jnp.float32)
    pre_up = jnp.dot(in_rows, w_up, preferred_element_type=jnp.float32)
    sigmoid_gate = jax.nn.sigmoid(pre_gate)
    activated = pre_gate * sigmoid_gate
    hidden = (activated * pre_up).astype(jnp.bfloat16)
    pre_gate, pre_up, sigmoid_gate, activated, hidden = (
        pre_gate,
        pre_up,
        sigmoid_gate,
        activated,
        hidden,
    )
    scaled = (
        recv_coeffs.reshape(num_ep * CAP)[:, None]
        * recv_grads.reshape(num_ep * CAP, width).astype(jnp.float32)
    ).astype(jnp.bfloat16)
    d_hidden = jnp.einsum("rd,hd->rh", scaled, w_down, preferred_element_type=jnp.float32)
    weight_grad = jnp.einsum("rh,rd->hd", hidden, scaled, preferred_element_type=jnp.float32)
    d_gate = (d_hidden * pre_up * sigmoid_gate * (1.0 + pre_gate * (1.0 - sigmoid_gate))).astype(
        jnp.bfloat16
    )
    d_up = (d_hidden * activated).astype(jnp.bfloat16)
    partial_value = jnp.einsum("rh,dh->rd", d_gate, w_gate, preferred_element_type=jnp.float32)
    partial_value = (
        partial_value + jnp.einsum("rh,dh->rd", d_up, w_up, preferred_element_type=jnp.float32)
    ).astype(jnp.bfloat16)
    returned = lax.all_to_all(
        partial_value.reshape(num_ep, CAP, width), "ep", split_axis=0, concat_axis=0, tiled=True
    )
    combine = jnp.broadcast_to(
        select_mask.reshape(slot_count, 1, CAP, tok_count), (slot_count, QUARTERS, CAP, tok_count)
    )
    combine = combine.reshape(num_ep * CAP, tok_count).astype(jnp.bfloat16)
    token_grad = jnp.einsum(
        "kt,kd->td",
        combine,
        returned.reshape(num_ep * CAP, width),
        preferred_element_type=jnp.float32,
    ).astype(jnp.bfloat16)
    ep_index = lax.axis_index("ep")
    my_cand = lax.dynamic_index_in_dim(placement[0], ep_index // QUARTERS, 0, keepdims=False)
    cand_mask = (jnp.arange(CANDS, dtype=jnp.int32) == my_cand).astype(jnp.float32)
    cand_grads = cand_mask[:, None, None] * weight_grad[None]
    totals = lax.psum(cand_grads.astype(jnp.bfloat16), "grp").astype(jnp.float32)
    full_first, full_second = (
        lax.all_gather(moment_first.astype(jnp.bfloat16), "grp", axis=2, tiled=True).astype(
            moment_first.dtype
        ),
        lax.all_gather(moment_second.astype(jnp.bfloat16), "grp", axis=2, tiled=True).astype(
            moment_second.dtype
        ),
    )
    share_cols = moment_first.shape[2]
    share_start = lax.axis_index("grp") * share_cols
    new_first, new_second = moments(
        lax.dynamic_slice_in_dim(totals, share_start, share_cols, 2), moment_first, moment_second
    )
    own_grad = lax.dynamic_index_in_dim(totals, my_cand, 0, keepdims=True)
    own_first = lax.dynamic_index_in_dim(full_first, my_cand, 0, keepdims=True)
    own_second = lax.dynamic_index_in_dim(full_second, my_cand, 0, keepdims=True)
    copy_first, copy_second = moments(own_grad, own_first, own_second)
    step_dir = direction(copy_first, copy_second).astype(jnp.bfloat16)
    return (token_grad, step_dir, new_first, new_second)


def solution(mesh):
    return jax.shard_map(
        body,
        mesh=mesh,
        in_specs=(
            P(("grp", "ep"), None),
            P(("grp", "ep"), None),
            P(("grp", "ep"), None),
            P("grp", None),
            P("grp", None, "ep"),
            P("grp", None, "ep"),
            P("grp", "ep", None),
            P(("grp", "ep"), None),
            P(None, "ep", "grp"),
            P(None, "ep", "grp"),
        ),
        out_specs=(
            P(("grp", "ep"), None),
            P("grp", "ep", None),
            P(None, "ep", "grp"),
            P(None, "ep", "grp"),
        ),
        check_vma=False,
    )
```

profile of v0, /device:TPU:8, one launch (start us, length us, event | category | flops | bytes accessed | tf_op | source)
XLA Modules:
  0.0 526.5 jit_solution(9174069582011565920)
XLA Ops:
  8.0 0.8 compare_reduce_fusion
  8.7 0.8 fusion.24
  9.6 1.2 reduce-window.6
  11.9 5.8 %all-to-all-start = ((bf16[16,1,24]{2,1,0:T(2,128)(2,1)}), bf16[16,1,24]{2,1,0:T(2,128)(2,1)S(1)}, u32[]{:S(2)}, u32[]{:S(2)}) async-start(bf16[16,1,24]{2,1,0:T(2,128)(2,1)} %copy.29), calls=%async_computation | async-start | bytes 16384 | tf_op jit(solution)/shard_map/all_to_all | solution.py:78
  17.9 1.8 convolution_convert_fusion.1
  19.7 2.6 all-to-all-done
  22.3 2.1 broadcast_in_dim.53
  24.4 5.7 %all-to-all-start.2 = ((bf16[16,24,4096]{2,1,0:T(8,128)(2,1)}), bf16[16,24,4096]{2,1,0:T(8,128)(2,1)}, u32[]{:S(2)}, u32[]{:S(2)}) async-start(bf16[16,24,4096]{2,1,0:T(8,128)(2,1)} %bitcast.62), calls=%async_computation.2 | async-start | bytes 6291456 | tf_op jit(solution)/shard_map/all_to_all | solution.py:76
  30.1 1.8 convolution_convert_fusion.2
  31.9 39.9 %all-to-all-done.2 = bf16[16,24,4096]{2,1,0:T(8,128)(2,1)} async-done(((bf16[16,24,4096]{2,1,0:T(8,128)(2,1)}), bf16[16,24,4096]{2,1,0:T(8,128)(2,1)}, u32[]{:S(2)}, u32[]{:S(2)}) %all-to-all-start.2) | async-done | bytes 3145760 | tf_op jit(solution)/shard_map/all_to_all | solution.py:76
  71.8 2.1 broadcast_in_dim.29
  73.8 5.4 %all-to-all-start.1 = ((bf16[16,24,4096]{2,1,0:T(8,128)(2,1)}), bf16[16,24,4096]{2,1,0:T(8,128)(2,1)}, u32[]{:S(2)}, u32[]{:S(2)}) async-start(bf16[16,24,4096]{2,1,0:T(8,128)(2,1)} %bitcast.60), calls=%async_computation.1 | async-start | bytes 6291456 | tf_op jit(solution)/shard_map/all_to_all | solution.py:77
  80.7 3.1 fusion.9
  83.7 3.8 fusion.12
  87.5 33.3 %all-to-all-done.1 = bf16[16,24,4096]{2,1,0:T(8,128)(2,1)} async-done(((bf16[16,24,4096]{2,1,0:T(8,128)(2,1)}), bf16[16,24,4096]{2,1,0:T(8,128)(2,1)}, u32[]{:S(2)}, u32[]{:S(2)}) %all-to-all-start.1) | async-done | bytes 3145760 | tf_op jit(solution)/shard_map/all_to_all | solution.py:77
  120.8 2.9 fusion
  123.8 1.0 fusion.18
  124.8 2.3 multiply_convert_fusion
  127.1 180.8 %all-reduce.3.cloned.1.call-done = bf16[2,192,4096]{2,1,0:T(8,128)(2,1)} async-done(((bf16[2,192,4096]{2,1,0:T(8,128)(2,1)}), bf16[2,192,4096]{2,1,0:T(8,128)(2,1)}) %all-reduce.3.cloned.1.call-update) | async-done | bytes 3145744 | tf_op jit(solution)/shard_map/psum | solution.py:126
  308.0 2.7 convert_element_type.124
  310.7 2.7 copy-done.1
  313.4 1.1 fusion.16
  315.2 3.0 multiply_convert_fusion.1
  318.3 1.2 fusion.14
  319.5 1.1 fusion.7
  320.6 2.7 add_convert_fusion
  323.3 6.4 %all-to-all-start.3 = ((bf16[16,24,4096]{2,1,0:T(8,128)(2,1)}), bf16[16,24,4096]{2,1,0:T(8,128)(2,1)}, u32[]{:S(2)}, u32[]{:S(2)}) async-start(bf16[16,24,4096]{2,1,0:T(8,128)(2,1)} %bitcast.61), calls=%async_computation.3 | async-start | bytes 6291456 | tf_op jit(solution)/shard_map/all_to_all | solution.py:109
  331.6 39.6 %all-to-all-done.3 = bf16[16,24,4096]{2,1,0:T(8,128)(2,1)} async-done(((bf16[16,24,4096]{2,1,0:T(8,128)(2,1)}), bf16[16,24,4096]{2,1,0:T(8,128)(2,1)}, u32[]{:S(2)}, u32[]{:S(2)}) %all-to-all-start.3) | async-done | bytes 3145760 | tf_op jit(solution)/shard_map/all_to_all | solution.py:109
  371.3 4.1 convolution_convert_fusion
  375.4 44.3 %all-gather.3.cloned.1.call-done = bf16[2,192,4096]{2,1,0:T(8,128)(2,1)} async-done(((bf16[2,192,256]{2,1,0:T(8,128)(2,1)}), bf16[2,192,4096]{2,1,0:T(8,128)(2,1)}) %all-gather.3.cloned.1.call-update) | async-done | bytes 3145744 | tf_op jit(solution)/shard_map/all_gather | solution.py:128
  419.7 94.2 %all-gather.5.cloned.1.call-done = bf16[2,192,4096]{2,1,0:T(8,128)(2,1)} async-done(((bf16[2,192,256]{2,1,0:T(8,128)(2,1)}), bf16[2,192,4096]{2,1,0:T(8,128)(2,1)}) %all-gather.5.cloned.1.call-update) | async-done | bytes 3145744 | tf_op jit(solution)/shard_map/all_gather | solution.py:131
  513.8 6.1 %fusion.6 = bf16[1,192,4096]{2,1,0:T(8,128)(2,1)} fusion(f32[2,192,4096]{2,1,0:T(8,128)} %copy-done.1, s32[]{:T(128)S(6)} %select_n.25, bf16[2,192,4096]{2,1,0:T(8,128)(2,1)} %all-gather.5.cloned.1.call-done, bf16[2,192,4096]{2,1,0:T(8,128)(2,1)} %all-gather.3.cloned.1.call-done), kind=kLoop, calls=%fused_computation.14 | loop fusion | flops 10223616 | bytes 7864324 | tf_op jit(solution)/shard_map/convert_element_type | solution.py:144
  (47 shorter events, 4.4 us)
Async XLA Ops:
  7.2 73.5 %copy-start = (bf16[1,4096,192]{1,2,0:T(8,128)(2,1)S(1)}, bf16[1,4096,192]{1,2,0:T(8,128)(2,1)}, u32[]{:S(2)}) copy-start(bf16[1,4096,192]{1,2,0:T(8,128)(2,1)} %param.14) | copy-start | bytes 4718596
  11.9 10.4 %all-to-all-start = ((bf16[16,1,24]{2,1,0:T(2,128)(2,1)}), bf16[16,1,24]{2,1,0:T(2,128)(2,1)S(1)}, u32[]{:S(2)}, u32[]{:S(2)}) async-start(bf16[16,1,24]{2,1,0:T(2,128)(2,1)} %copy.29), calls=%async_computation | async-start | bytes 16384 | tf_op jit(solution)/shard_map/all_to_all | solution.py:78
  24.4 47.4 %all-to-all-start.2 = ((bf16[16,24,4096]{2,1,0:T(8,128)(2,1)}), bf16[16,24,4096]{2,1,0:T(8,128)(2,1)}, u32[]{:S(2)}, u32[]{:S(2)}) async-start(bf16[16,24,4096]{2,1,0:T(8,128)(2,1)} %bitcast.62), calls=%async_computation.2 | async-start | bytes 6291456 | tf_op jit(solution)/shard_map/all_to_all | solution.py:76
  73.8 5.4 %copy-start.8 = (s32[1,4]{1,0:T(1,128)S(1)}, s32[1,4]{1,0:T(1,128)}, u32[]{:S(2)}) copy-start(s32[1,4]{1,0:T(1,128)} %param.13) | copy-start | bytes 52
  73.8 47.0 %all-to-all-start.1 = ((bf16[16,24,4096]{2,1,0:T(8,128)(2,1)}), bf16[16,24,4096]{2,1,0:T(8,128)(2,1)}, u32[]{:S(2)}, u32[]{:S(2)}) async-start(bf16[16,24,4096]{2,1,0:T(8,128)(2,1)} %bitcast.60), calls=%async_computation.1 | async-start | bytes 6291456 | tf_op jit(solution)/shard_map/all_to_all | solution.py:77
  79.2 4.5 copy-start.2
  79.2 228.7 %all-reduce.3.cloned.1.call-start = ((), (), s32[]{:S(2)}) async-start(), calls=%async_computation.5 | async-start | bytes 6291456 | tf_op jit(solution)/shard_map/psum | solution.py:126
  120.8 2.9 copy-start.3
  127.1 292.6 %all-gather.3.cloned.1.call-start = ((), (), s32[]{:S(2)}) async-start(), calls=%async_computation.4 | async-start | bytes 3342336 | tf_op jit(solution)/shard_map/all_gather | solution.py:128
  308.0 5.4 %copy-start.5 = (f32[2,192,256]{2,1,0:T(8,128)S(1)}, f32[2,192,256]{2,1,0:T(8,128)}, u32[]{:S(2)}) copy-start(f32[2,192,256]{2,1,0:T(8,128)} %param.19) | copy-start | bytes 1179652
  308.0 5.4 %copy-start.6 = (f32[2,192,256]{2,1,0:T(8,128)S(1)}, f32[2,192,256]{2,1,0:T(8,128)}, u32[]{:S(2)}) copy-start(f32[2,192,256]{2,1,0:T(8,128)} %param.18) | copy-start | bytes 1179652
  310.7 2.7 copy-start.1
  314.5 199.4 %all-gather.5.cloned.1.call-start = ((), (), s32[]{:S(2)}) async-start(), calls=%async_computation.6 | async-start | bytes 3342336 | tf_op jit(solution)/shard_map/all_gather | solution.py:131
  315.2 3.0 copy-start.7
  318.2 1.2 copy-start.4
  323.3 48.0 %all-to-all-start.3 = ((bf16[16,24,4096]{2,1,0:T(8,128)(2,1)}), bf16[16,24,4096]{2,1,0:T(8,128)(2,1)}, u32[]{:S(2)}, u32[]{:S(2)}) async-start(bf16[16,24,4096]{2,1,0:T(8,128)(2,1)} %bitcast.61), calls=%async_computation.3 | async-start | bytes 6291456 | tf_op jit(solution)/shard_map/all_to_all | solution.py:109
Sparse Core Ops, SparseCore 0:
  127.2 180.7 all-reduce.2
  314.6 105.0 all-gather.2
  422.2 91.6 all-gather.4
where the time goes:
time: 528 us; the launch traced here: 526 us
  waiting for transfers between devices  436 us (83%)
  starting transfers between devices  23.3 us (4%)
  other arithmetic  22.7 us (4%)
  matrix products  20.5 us (4%)
  between operations  15.9 us (3%)
  local copies, waits for them, and re-layouts  8.51 us (2%)
    psum x1, waiting for transfers between devices, body(): lax.psum(cand_grads.astype(jnp.bfloat16), 'grp').astype(jnp.float32)  181 us
    all_gather x1, waiting for transfers between devices, body(): lax.all_gather(moment_second.astype(jnp.bfloat16), 'grp', axis=2, tiled=T...  94.2 us
    all_gather x1, waiting for transfers between devices, body(): lax.all_gather(moment_first.astype(jnp.bfloat16), 'grp', axis=2, tiled=True)  44.3 us
    all_to_all x1, waiting for transfers between devices, body(): lax.all_to_all(spread(send_tokens), 'ep', split_axis=0, concat_axis=0, ti...  39.9 us
    all_to_all x1, waiting for transfers between devices, body(): lax.all_to_all(partial_value.reshape(num_ep, CAP, width), 'ep', split_axi...  39.6 us
    all_to_all x1, waiting for transfers between devices, body(): lax.all_to_all(spread(send_grads), 'ep', split_axis=0, concat_axis=0, til...  33.3 us
  transfers between devices with their start and end apart: 7, of which 7 were waited for; matrix products, arithmetic and copies ran while one was open for 5% of the time, Pallas kernels for 0%

commit v1 on v0

v1 whole, which is shorter than its diff:
```python
import math

import jax
import jax.numpy as jnp
from jax import lax
from jax.experimental import pallas as pl
from jax.experimental.pallas import tpu as pltpu
from jax.sharding import PartitionSpec as P

MESH = pl.DeviceIdType.MESH
F32 = jnp.float32
BF16 = jnp.bfloat16

D = 4096
HALF = 2048
TOK = 192
HU = 192
CAP = 24
PAIR = 2 * CAP
SLOTS = 4
CHIPS = 8
NX = 4
NZ = 8
SHARE = 256
ROWS = CHIPS * PAIR
CH = 512

beta_one = 0.9
beta_two = 0.999
adam_eps = 1e-08
first_fix = 1.0 - math.exp(1000.0 * math.log(0.9))
second_fix = 1.0 - math.exp(1000.0 * math.log(0.999))

OFFS = [(dy, dx) for dx in (2, 1, 3, 0) for dy in (1, 0) if (dy, dx) != (0, 0)]
NO = len(OFFS)
NT = (((1,), (1,)), ((), ()))


def body(
    tok, ids, prb, plc, wg, wu, wd, og, m1, m2,
    tg_out, sd_out, nf_out, ns_out,
    tokH, grdH, idsH, prbH, hm, cm, sel_t, snd_t, snd_g, xt, xg,
    wgv, wuv, wdv, m1v, m2v, hid_t, dgv, duv,
    p_snd, p_rcv, p_own, r_snd, r_rcv, tgv,
    mine, theirs, wy_snd, wy_rcv, w_own,
    rm_snd, rm_rcv, rp_snd, rp_rcv, dall, ds, dy,
    lsem, s_in, r_in, s_t, r_t, f_t, g_t, s_g, r_g, f_g, g_g,
    s_p, r_p, s_r, r_r, s_tg, r_tg,
    s_c, r_c, s_y, r_y, s_m, r_m, s_q, r_q, s_am, r_am, s_ap, r_ap, s_d, r_d, l_d,
):
    g = lax.axis_index("grp")
    e = lax.axis_index("ep")
    z, yh = g // 2, lax.rem(g, 2)
    q, k = e // 2, lax.rem(e, 2)
    yl, x = q // NX, lax.rem(q, NX)
    slot = q // 2
    sib = {"grp": g, "ep": q * 2 + 1 - k}
    ypart = {"grp": z * 2 + 1 - yh, "ep": e}
    zup = {"grp": lax.rem(z + 1, NZ) * 2 + yh, "ep": e}
    zdn = {"grp": lax.rem(z + NZ - 1, NZ) * 2 + yh, "ep": e}

    def chip(off, sign):
        return lax.rem(yl + off[0], 2) * NX + lax.rem(x + sign * off[1] + NX, NX)

    def remote(src, dst, ssem, rsem, to):
        return pltpu.make_async_remote_copy(
            src_ref=src, dst_ref=dst, send_sem=ssem, recv_sem=rsem, device_id=to,
            device_id_type=MESH,
        )

    def cols(i):
        return pl.ds(pl.multiple_of(i * SHARE, SHARE), SHARE)

    mine_cols = pl.ds(pl.multiple_of(k * HALF, HALF), HALF)
    other_cols = pl.ds(pl.multiple_of((1 - k) * HALF, HALF), HALF)

    local = [
        pltpu.make_async_copy(ids, idsH.at[k], lsem.at[0]),
        pltpu.make_async_copy(prb, prbH.at[k], lsem.at[1]),
        pltpu.make_async_copy(tok.at[:, mine_cols], tokH.at[k], lsem.at[2]),
        pltpu.make_async_copy(og.at[:, mine_cols], grdH.at[k], lsem.at[3]),
    ]
    later = [
        pltpu.make_async_copy(wg.at[0], wgv, lsem.at[4]),
        pltpu.make_async_copy(wu.at[0], wuv, lsem.at[5]),
        pltpu.make_async_copy(wd.at[0], wdv, lsem.at[6]),
        pltpu.make_async_copy(m1, m1v, lsem.at[7]),
        pltpu.make_async_copy(m2, m2v, lsem.at[8]),
    ]
    for cp in local + later:
        cp.start()
    mine[...] = jnp.zeros((8, 128), jnp.int32) + plc[0, slot]

    barrier = pltpu.get_barrier_semaphore()
    greet = [sib, ypart, zup, zdn]
    greet += [{"grp": g, "ep": chip(o, 1) * 2 + k} for o in OFFS]
    for to in greet:
        pl.semaphore_signal(barrier, inc=1, device_id=to, device_id_type=MESH)
    pl.semaphore_wait(barrier, len(greet))

    swap = [
        remote(ids, idsH.at[k], s_in.at[0], r_in.at[0], sib),
        remote(prb, prbH.at[k], s_in.at[1], r_in.at[1], sib),
        remote(tok.at[:, other_cols], tokH.at[k], s_in.at[2], r_in.at[2], sib),
        remote(og.at[:, other_cols], grdH.at[k], s_in.at[3], r_in.at[3], sib),
    ]
    for cp in swap:
        cp.start()
    cand_copy = remote(mine, theirs, s_c.at[0], r_c.at[0], ypart)
    cand_copy.start()

    for i in (0, 1):
        local[i].wait()
        swap[i].wait()
    lane = lax.broadcasted_iota(jnp.int32, (TOK, 128), 1)
    for kk in (0, 1):
        id_rows, prob_rows = idsH[kk], prbH[kk]
        hits = jnp.zeros((TOK, 128), F32)
        coefs = jnp.zeros((TOK, 128), F32)
        for s in range(SLOTS):
            match = id_rows == plc[0, s] * SLOTS + s
            hit = jnp.max(jnp.where(match, 1.0, 0.0), axis=1, keepdims=True)
            coef = jnp.sum(jnp.where(match, prob_rows, 0.0), axis=1, keepdims=True)
            hits = jnp.where(lane == s, hit, hits)
            coefs = jnp.where(lane == s, coef, coefs)
        hm[kk * TOK : (kk + 1) * TOK, :] = hits
        cm[kk * TOK : (kk + 1) * TOK, :] = coefs
    hit_r = jnp.transpose(hm[...])[0:8]
    coef_r = jnp.transpose(cm[...])[0:8]
    row = lax.broadcasted_iota(jnp.int32, (2 * TOK, 2 * TOK), 0)
    col = lax.broadcasted_iota(jnp.int32, (2 * TOK, 2 * TOK), 1)
    before = (row < col) & ((row >= TOK) == (col >= TOK))
    before = jnp.where(before, 1.0, 0.0).astype(BF16)
    rank_r = jnp.dot(hit_r.astype(BF16), before, preferred_element_type=F32)
    r48 = lax.broadcasted_iota(jnp.int32, (PAIR, 2 * TOK), 0)
    t48 = lax.broadcasted_iota(jnp.int32, (PAIR, 2 * TOK), 1)
    same = (r48 >= CAP) == (t48 >= TOK)
    place = jnp.where(r48 >= CAP, r48 - CAP, r48).astype(F32)
    picks, scales = [], []
    for s in range(SLOTS):
        ok = same & (hit_r[s : s + 1] > 0.5) & (rank_r[s : s + 1] == place)
        pick = jnp.where(ok, 1.0, 0.0)
        picks.append(pick)
        scales.append(jnp.sum(pick * coef_r[s : s + 1], axis=1, keepdims=True))
    pick_all = jnp.concatenate(picks, axis=0)
    scale_all = jnp.concatenate(scales, axis=0)
    sel_t[...] = jnp.transpose(pick_all).astype(BF16)
    pick_all = pick_all.astype(BF16)

    def select(src, out, scale):
        for c in range(0, HALF, CH):
            rows = src[:, :, c : c + CH].reshape(2 * TOK, CH)
            got = jnp.dot(pick_all, rows, preferred_element_type=F32)
            if scale is not None:
                got = got * scale
            out[:, :, c : c + CH] = got.astype(BF16).reshape(SLOTS, PAIR, CH)

    def dispatch(out, dst, ssem, rsem, fs, fr):
        sends = []
        for i, o in enumerate(OFFS):
            there = chip(o, 1)
            sends.append(remote(out.at[there // 2], dst.at[k, q], ssem.at[i], rsem.at[i],
                                {"grp": g, "ep": there * 2 + k}))
        own = pltpu.make_async_copy(out.at[slot], dst.at[k, q], ssem.at[NO])
        across = remote(out.at[slot], dst.at[k, q], fs.at[NO], fr.at[NO], sib)
        for cp in sends:
            cp.start()
        own.start()
        across.start()
        return sends, own, across

    def arrive(sends, own, across, dst, fs, fr):
        forwards = []
        for i in reversed(range(NO)):
            here = chip(OFFS[i], -1)
            sends[i].wait_recv()
            cp = remote(dst.at[k, here], dst.at[k, here], fs.at[i], fr.at[i], sib)
            cp.start()
            forwards.append(cp)
        for cp in forwards:
            cp.wait()
        across.wait()
        own.wait()
        for cp in sends:
            cp.wait_send()

    local[2].wait()
    swap[2].wait()
    select(tokH, snd_t, None)
    tok_copies = dispatch(snd_t, xt, s_t, r_t, f_t, g_t)
    local[3].wait()
    swap[3].wait()
    select(grdH, snd_g, scale_all)
    grd_copies = dispatch(snd_g, xg, s_g, r_g, f_g, g_g)
    for cp in later:
        cp.wait()
    cand_copy.wait()

    arrive(*tok_copies, xt, f_t, g_t)
    pre_gate = jnp.zeros((ROWS, HU), F32)
    pre_up = jnp.zeros((ROWS, HU), F32)
    for c in range(0, D, CH):
        rows = xt[c // HALF, :, :, c % HALF : c % HALF + CH].reshape(ROWS, CH)
        pre_gate += jnp.dot(rows, wgv[c : c + CH, :], preferred_element_type=F32)
        pre_up += jnp.dot(rows, wuv[c : c + CH, :], preferred_element_type=F32)
    sig = jax.nn.sigmoid(pre_gate)
    act = pre_gate * sig
    hid_t[...] = jnp.transpose(act * pre_up).astype(BF16)

    arrive(*grd_copies, xg, f_g, g_g)

    def grad_share(zd, yd):
        share = zd * 2 + yd
        at = pl.ds(pl.multiple_of(lax.rem(share, 8) * SHARE, SHARE), SHARE)
        rows = xg[share // 8, :, :, at].reshape(ROWS, SHARE)
        return jnp.dot(hid_t[...], rows, preferred_element_type=F32).astype(BF16)

    order = [4, 3, 5, 2, 6, 1, 7, 0]
    y_copies = []
    for n, up in enumerate(order):
        wy_snd[n] = grad_share(lax.rem(z + up, NZ), 1 - yh)
        cp = remote(wy_snd.at[n], wy_rcv.at[n], s_y.at[n], r_y.at[n], ypart)
        cp.start()
        y_copies.append(cp)

    d_hidden = jnp.zeros((ROWS, HU), F32)
    for c in range(0, D, CH):
        rows = xg[c // HALF, :, :, c % HALF : c % HALF + CH].reshape(ROWS, CH)
        d_hidden += lax.dot_general(rows, wdv[:, c : c + CH], NT, preferred_element_type=F32)
    dgv[...] = (d_hidden * pre_up * sig * (1.0 + pre_gate * (1.0 - sig))).astype(BF16)
    duv[...] = (d_hidden * act).astype(BF16)

    def partial(start):
        at = pl.ds(pl.multiple_of(start, CH), CH)
        got = lax.dot_general(dgv[...], wgv[at, :], NT, preferred_element_type=F32)
        return got + lax.dot_general(duv[...], wuv[at, :], NT, preferred_element_type=F32)

    for c in range(0, HALF, CH):
        got = partial((1 - k) * HALF + c)
        p_snd[:, :, c : c + CH] = got.astype(BF16).reshape(CHIPS, PAIR, CH)
    p_copy = remote(p_snd, p_rcv, s_p.at[0], r_p.at[0], sib)
    p_copy.start()
    for c in range(0, HALF, CH):
        p_own[:, :, c : c + CH] = partial(k * HALF + c).reshape(CHIPS, PAIR, CH)
    for n, up in enumerate(order):
        w_own[n] = grad_share(lax.rem(z + up, NZ), yh)
    p_copy.wait()
    r_copies = []
    for i, o in enumerate(OFFS):
        there = chip(o, 1)
        r_snd[i] = (p_own[there] + p_rcv[there].astype(F32)).astype(BF16)
        cp = remote(r_snd.at[i], r_rcv.at[lax.rem(q, 2), slot], s_r.at[i], r_r.at[i],
                    {"grp": g, "ep": there * 2 + k})
        cp.start()
        r_copies.append(cp)
    r_rcv[lax.rem(q, 2), slot] = (p_own[q] + p_rcv[q].astype(F32)).astype(BF16)

    cand_a = mine[0:1, 0:1]
    cand_b = theirs[0:1, 0:1]

    def both(n):
        y_copies[n].wait_recv()
        a, b = w_own[n].astype(F32), wy_rcv[n].astype(F32)
        return [
            jnp.where(cand_a == c, a, 0.0) + jnp.where(cand_b == c, b, 0.0) for c in (0, 1)
        ]

    def ring(snd, rcv, ssem, rsem, t, n, to, prev):
        terms = both(n)
        if prev is not None:
            prev.wait_recv()
        for c in (0, 1):
            value = terms[c]
            if prev is not None:
                value = value + rcv[t - 1, c].astype(F32)
            snd[t, c] = value.astype(BF16)
        cp = remote(snd.at[t], rcv.at[t], ssem.at[t], rsem.at[t], to)
        cp.start()
        return cp

    downs, ups = [], []
    for t in range(4):
        n = order.index((4 + t) % NZ)
        downs.append(ring(rm_snd, rm_rcv, s_m, r_m, t, n, zdn, downs[-1] if downs else None))
        if t < 3:
            n = order.index(3 - t)
            ups.append(ring(rp_snd, rp_rcv, s_q, r_q, t, n, zup, ups[-1] if ups else None))
    total = both(order.index(0))
    ups[-1].wait_recv()
    total = [total[c] + rp_rcv[2, c].astype(F32) for c in (0, 1)]
    downs[-1].wait_recv()
    total = [total[c] + rm_rcv[3, c].astype(F32) for c in (0, 1)]
    for c in (0, 1):
        grad = total[c]
        first = beta_one * m1v[c] + (1.0 - beta_one) * grad
        second = beta_two * m2v[c] + (1.0 - beta_two) * grad * grad
        m1v[c] = first
        m2v[c] = second
        step = first / first_fix / (jnp.sqrt(second / second_fix) + adam_eps)
        dall[z, c] = step.astype(BF16)
    outs = [
        pltpu.make_async_copy(m1v, nf_out, lsem.at[0]),
        pltpu.make_async_copy(m2v, ns_out, lsem.at[1]),
    ]
    for cp in outs:
        cp.start()

    d_copies = []

    def use(n, zo):
        for buf, cand in ((dy, cand_b), (ds, cand_a)):
            buf[n] = jnp.where(cand == 0, dall[zo, 0].astype(F32), dall[zo, 1].astype(F32)).astype(BF16)
        at = cols(zo * 2 + yh)
        cp = remote(dy.at[n], sd_out.at[0, :, at], s_d.at[n], r_d.at[n], ypart)
        cp.start()
        d_copies.append(cp)
        cp = pltpu.make_async_copy(ds.at[n], sd_out.at[0, :, at], l_d.at[n])
        cp.start()
        outs.append(cp)

    def pass_on(zo, ssem, rsem, t, to):
        cp = remote(dall.at[zo], dall.at[zo], ssem.at[t], rsem.at[t], to)
        cp.start()
        return cp

    a_up = [pass_on(z, s_ap, r_ap, 0, zup)]
    a_dn = [pass_on(z, s_am, r_am, 0, zdn)]
    use(0, z)

    def combine():
        for cp in r_copies:
            cp.wait_recv()
        for c in range(0, HALF, CH):
            got = jnp.zeros((2 * TOK, CH), F32)
            for ab in (0, 1):
                rows = r_rcv[ab, :, :, c : c + CH].reshape(SLOTS * PAIR, CH)
                got += jnp.dot(sel_t[...], rows, preferred_element_type=F32)
            tgv[:, :, c : c + CH] = got.astype(BF16).reshape(2, TOK, CH)
        across = remote(tgv.at[1 - k], tg_out.at[:, mine_cols], s_tg.at[0], r_tg.at[0], sib)
        across.start()
        own = pltpu.make_async_copy(tgv.at[k], tg_out.at[:, mine_cols], lsem.at[2])
        own.start()
        return across, own

    for t in range(4):
        below = lax.rem(z + NZ - t - 1, NZ)
        a_up[t].wait_recv()
        if t < 3:
            a_up.append(pass_on(below, s_ap, r_ap, t + 1, zup))
        use(1 + t, below)
        if t < 3:
            above = lax.rem(z + t + 1, NZ)
            a_dn[t].wait_recv()
            if t < 2:
                a_dn.append(pass_on(above, s_am, r_am, t + 1, zdn))
            use(5 + t, above)
        if t == 1:
            tg_copy, tg_own = combine()

    tg_copy.wait()
    tg_own.wait()
    for cp in d_copies:
        cp.wait()
    for cp in outs:
        cp.wait()
    for cp in y_copies + r_copies + downs + ups + a_up + a_dn:
        cp.wait_send()


def step(tokens, expert_ids, gate_probs, placement, gate_weight, up_weight, down_weight,
         out_grad, moment_first, moment_second):
    def vm(*shape, dtype=BF16):
        return pltpu.VMEM(shape, dtype)

    dma = lambda n: pltpu.SemaphoreType.DMA((n,))
    anywhere = pl.BlockSpec(memory_space=pl.ANY)
    outs = pl.pallas_call(
        body,
        out_shape=(
            jax.ShapeDtypeStruct((TOK, D), BF16),
            jax.ShapeDtypeStruct((1, HU, D), BF16),
            jax.ShapeDtypeStruct((2, HU, SHARE), F32),
            jax.ShapeDtypeStruct((2, HU, SHARE), F32),
        ),
        in_specs=[anywhere] * 3 + [pl.BlockSpec(memory_space=pltpu.SMEM)] + [anywhere] * 6,
        out_specs=(anywhere,) * 4,
        scratch_shapes=[
            vm(2, TOK, HALF), vm(2, TOK, HALF),
            vm(2, TOK, 8, dtype=jnp.int32), vm(2, TOK, 8, dtype=F32),
            vm(2 * TOK, 128, dtype=F32), vm(2 * TOK, 128, dtype=F32),
            vm(2 * TOK, SLOTS * PAIR),
            vm(SLOTS, PAIR, HALF), vm(SLOTS, PAIR, HALF),
            vm(2, CHIPS, PAIR, HALF), vm(2, CHIPS, PAIR, HALF),
            vm(D, HU), vm(D, HU), vm(HU, D),
            vm(2, HU, SHARE, dtype=F32), vm(2, HU, SHARE, dtype=F32),
            vm(HU, ROWS), vm(ROWS, HU), vm(ROWS, HU),
            vm(CHIPS, PAIR, HALF), vm(CHIPS, PAIR, HALF), vm(CHIPS, PAIR, HALF, dtype=F32),
            vm(NO, PAIR, HALF), vm(2, SLOTS, PAIR, HALF), vm(2, TOK, HALF),
            vm(8, 128, dtype=jnp.int32), vm(8, 128, dtype=jnp.int32),
            vm(NZ, HU, SHARE), vm(NZ, HU, SHARE), vm(NZ, HU, SHARE),
            vm(4, 2, HU, SHARE), vm(4, 2, HU, SHARE), vm(3, 2, HU, SHARE), vm(3, 2, HU, SHARE),
            vm(NZ, 2, HU, SHARE), vm(NZ, HU, SHARE), vm(NZ, HU, SHARE),
            dma(9), dma(4), dma(4),
            dma(8), dma(8), dma(8), dma(8), dma(8), dma(8), dma(8), dma(8),
            dma(1), dma(1), dma(8), dma(8), dma(1), dma(1),
            dma(1), dma(1), dma(8), dma(8), dma(4), dma(4), dma(4), dma(4),
            dma(4), dma(4), dma(4), dma(4), dma(8), dma(8), dma(8),
        ],
        compiler_params=pltpu.CompilerParams(
            collective_id=0, has_side_effects=True, vmem_limit_bytes=60 * 2**20
        ),
    )(tokens, expert_ids, gate_probs, placement, gate_weight, up_weight, down_weight,
      out_grad, moment_first, moment_second)
    return outs


def solution(mesh):
    return jax.shard_map(
        step,
        mesh=mesh,
        in_specs=(
            P(("grp", "ep"), None),
            P(("grp", "ep"), None),
            P(("grp", "ep"), None),
            P("grp", None),
            P("grp", None, "ep"),
            P("grp", None, "ep"),
            P("grp", "ep", None),
            P(("grp", "ep"), None),
            P(None, "ep", "grp"),
            P(None, "ep", "grp"),
        ),
        out_specs=(
            P(("grp", "ep"), None),
            P("grp", "ep", None),
            P(None, "ep", "grp"),
            P(None, "ep", "grp"),
        ),
        check_vma=False,
    )
```

time: 528 us -> 138 us (0.26)
  the two profiles are of different devices: /device:TPU:8 before, /device:TPU:56 now
where the time goes in v1:
time: 138 us; the launch traced here: 137 us
  Pallas kernels  122 us (88%)
  local copies, waits for them, and re-layouts  14.9 us (11%)
    pallas_call x1, Pallas kernels, step(): pl.pallas_call(body, out_shape=(jax.ShapeDtypeStruct((TOK, D), BF16), jax...  122 us
    unnamed x16, local copies, waits for them, and re-layouts  14.9 us

profile of v1, /device:TPU:56, one launch (start us, length us, event | category | flops | bytes accessed | tf_op | source)
XLA Modules:
  0.0 137.5 jit_solution(5795007575890684974)
XLA Ops:
  0.6 1.5 %copy.14.ids = s32[192,8]{1,0:T(8,128)} copy(s32[192,8]{0,1:T(8,128)} %param.11) | data formatting | bytes 12288 | tf_op args[1]
  2.1 1.5 %copy.15.prb = f32[192,8]{1,0:T(8,128)} copy(f32[192,8]{0,1:T(8,128)} %param.12) | data formatting | bytes 12288 | tf_op args[2]
  3.5 0.0 copy-start
  3.5 3.9 %copy.16.wg = bf16[1,4096,192]{2,1,0:T(8,128)(2,1)} copy(bf16[1,4096,192]{1,2,0:T(8,128)(2,1)} %param.14) | data formatting | bytes 3145728 | tf_op args[4]
  7.5 0.0 copy-done
  7.5 2.5 %copy.17.wu = bf16[1,4096,192]{2,1,0:T(8,128)(2,1)} copy(bf16[1,4096,192]{1,2,0:T(8,128)(2,1)S(1)} %copy-done) | data formatting | bytes 3145728 | tf_op args[5]
  9.9 122.0 %shard_map.129 = (bf16[192,4096]{1,0:T(8,128)(2,1)}, bf16[1,192,4096]{2,1,0:T(8,128)(2,1)}, f32[2,192,256]{2,1,0:T(8,128)}, f32[2,192,256]{2,1,0:T(8,128)}) custom-call(bf16[192,4096]{1,0:T(8,128)(2,1)} %tok.1, s32[192,8]{1,0:T(8,128)} %copy.14.ids, f32[192,8]{1,0:T(8,128)} %copy.15.prb, s32[1,4]{1,0:T(1,128)} %plc.1, bf16[1,4096,192]{2,1,0:T(8,128)(2,1)} %copy.16.wg, ...), custom_call_target="tpu_custom_call" | custom-call | tf_op jit(solution)/shard_map/pallas_call | solution.py:377
  131.9 0.0 copy-start.1
  131.9 2.8 %copy.22 = bf16[192,4096]{1,0:T(8,128)(2,1)} copy(bf16[192,4096]{1,0:T(8,128)(2,1)} %get-tuple-element.8) | data formatting | bytes 3145728
  134.7 0.0 copy-done.1
  134.8 0.0 copy-start.3
  134.8 0.0 copy-start.2
  134.8 1.1 copy.23
  135.9 0.1 copy-done.3
  136.0 0.7 copy.24
  136.7 0.0 copy-done.2
  136.7 0.7 copy.25
Async XLA Ops:
  3.5 3.9 %copy-start = (bf16[1,4096,192]{1,2,0:T(8,128)(2,1)S(1)}, bf16[1,4096,192]{1,2,0:T(8,128)(2,1)}, u32[]{:S(2)}) copy-start(bf16[1,4096,192]{1,2,0:T(8,128)(2,1)} %param.15) | copy-start | bytes 4718596
  131.9 2.8 %copy-start.1 = (bf16[1,192,4096]{2,1,0:T(8,128)(2,1)S(1)}, bf16[1,192,4096]{2,1,0:T(8,128)(2,1)}, u32[]{:S(2)}) copy-start(bf16[1,192,4096]{2,1,0:T(8,128)(2,1)} %get-tuple-element.9) | copy-start | bytes 4718596
  134.8 1.2 copy-start.3
  134.8 2.0 %copy-start.2 = (f32[2,192,256]{2,1,0:T(8,128)S(1)}, f32[2,192,256]{2,1,0:T(8,128)}, u32[]{:S(2)}) copy-start(f32[2,192,256]{2,1,0:T(8,128)} %get-tuple-element.11) | copy-start | bytes 1179652

commit v2 on v1

v2 whole, which is shorter than its diff:
```python
import math

import jax
import jax.numpy as jnp
from jax import lax
from jax.experimental import pallas as pl
from jax.experimental.pallas import tpu as pltpu
from jax.sharding import PartitionSpec as P

MESH = pl.DeviceIdType.MESH
F32 = jnp.float32
BF16 = jnp.bfloat16

D = 4096
HALF = 2048
TOK = 192
HU = 192
CAP = 24
PAIR = 2 * CAP
SLOTS = 4
CHIPS = 8
NX = 4
NZ = 8
SHARE = 256
ROWS = CHIPS * PAIR
CH = 512

beta_one = 0.9
beta_two = 0.999
adam_eps = 1e-08
first_fix = 1.0 - math.exp(1000.0 * math.log(0.9))
second_fix = 1.0 - math.exp(1000.0 * math.log(0.999))

XD = (2, 1, 3)
NC = 4
NT = (((1,), (1,)), ((), ()))


def body(
    tok, ids, prb, plc, wg, wu, wd, og, m1, m2,
    tg_out, sd_out, nf_out, ns_out,
    tokH, grdH, idsH, prbH, sel_t, snd_t, snd_g, rel_t, rel_g, xt, xg,
    wgv, wuv, wdv, m1v, m2v, hid_t, dgv, duv,
    p_snd, p_rcv, p_own, r_snd, fin, relr, rel_s, rback, tgv,
    mine, theirs, wy_snd, wy_rcv, w_own,
    rm_snd, rm_rcv, rp_snd, rp_rcv, dall, dy,
    lsem, s_in, r_in,
    tl, tys, tyr, txs, txr, tfs, tfr, gl, gys, gyr, gxs, gxr, gfs, gfr,
    s_p, r_p, s_r, r_r, s_ry, r_ry, s_tg, r_tg,
    s_c, r_c, s_y, r_y, s_m, r_m, s_q, r_q, s_am, r_am, s_ap, r_ap, s_d, r_d,
):
    g = lax.axis_index("grp")
    e = lax.axis_index("ep")
    z, yh = g // 2, lax.rem(g, 2)
    q, k = e // 2, lax.rem(e, 2)
    yl, x = q // NX, lax.rem(q, NX)
    slot = q // 2
    row_slots, far_slots = yl * 2, (1 - yl) * 2
    side = x // 2
    q_far = (1 - yl) * NX + x
    sib = {"grp": g, "ep": q * 2 + 1 - k}
    far = {"grp": g, "ep": q_far * 2 + k}
    ypart = {"grp": z * 2 + 1 - yh, "ep": e}
    zup = {"grp": lax.rem(z + 1, NZ) * 2 + yh, "ep": e}
    zdn = {"grp": lax.rem(z + NZ - 1, NZ) * 2 + yh, "ep": e}
    x_of = [lax.rem(x + d, NX) for d in XD]
    x_from = [lax.rem(x - d + NX, NX) for d in XD]
    along = [{"grp": g, "ep": (yl * NX + xd) * 2 + k} for xd in x_of]

    def remote(src, dst, ssem, rsem, to):
        return pltpu.make_async_remote_copy(
            src_ref=src, dst_ref=dst, send_sem=ssem, recv_sem=rsem, device_id=to,
            device_id_type=MESH,
        )

    def cols(i):
        return pl.ds(pl.multiple_of(i * SHARE, SHARE), SHARE)

    mine_cols = pl.ds(pl.multiple_of(k * HALF, HALF), HALF)
    other_cols = pl.ds(pl.multiple_of((1 - k) * HALF, HALF), HALF)

    local = [
        pltpu.make_async_copy(ids, idsH.at[k], lsem.at[0]),
        pltpu.make_async_copy(prb, prbH.at[k], lsem.at[1]),
        pltpu.make_async_copy(tok.at[:, mine_cols], tokH.at[k], lsem.at[2]),
        pltpu.make_async_copy(og.at[:, mine_cols], grdH.at[k], lsem.at[3]),
    ]
    later = [
        pltpu.make_async_copy(wg.at[0], wgv, lsem.at[4]),
        pltpu.make_async_copy(wu.at[0], wuv, lsem.at[5]),
        pltpu.make_async_copy(wd.at[0], wdv, lsem.at[6]),
        pltpu.make_async_copy(m1, m1v, lsem.at[7]),
        pltpu.make_async_copy(m2, m2v, lsem.at[8]),
    ]
    for cp in local:
        cp.start()
    mine[...] = jnp.zeros((8, 128), jnp.int32) + plc[0, slot]

    barrier = pltpu.get_barrier_semaphore()
    greet = [sib, far, ypart, zup, zdn] + along
    for to in greet:
        pl.semaphore_signal(barrier, inc=1, device_id=to, device_id_type=MESH)
    pl.semaphore_wait(barrier, len(greet))

    swap = [
        remote(ids, idsH.at[k], s_in.at[0], r_in.at[0], sib),
        remote(prb, prbH.at[k], s_in.at[1], r_in.at[1], sib),
        remote(tok.at[:, other_cols], tokH.at[k], s_in.at[2], r_in.at[2], sib),
        remote(og.at[:, other_cols], grdH.at[k], s_in.at[3], r_in.at[3], sib),
    ]
    for cp in swap:
        cp.start()
    cand_copy = remote(mine, theirs, s_c.at[0], r_c.at[0], ypart)
    cand_copy.start()
    for cp in later:
        cp.start()

    for i in (0, 1):
        local[i].wait()
        swap[i].wait()
    row = lax.broadcasted_iota(jnp.int32, (TOK, TOK), 0)
    col = lax.broadcasted_iota(jnp.int32, (TOK, TOK), 1)
    before = jnp.where(row < col, 1.0, 0.0).astype(BF16)
    line = lax.broadcasted_iota(jnp.int32, (8, TOK), 0)
    r48 = lax.broadcasted_iota(jnp.int32, (PAIR, TOK), 0)
    place = jnp.where(r48 >= CAP, r48 - CAP, r48).astype(F32)
    pick_all = []
    scale_all = jnp.zeros((SLOTS * PAIR, 1), F32)
    for kk in (0, 1):
        id_rows, prob_rows = idsH[kk], prbH[kk]
        hits = jnp.zeros((8, TOK), F32)
        coefs = []
        for s in range(SLOTS):
            match = id_rows == plc[0, s] * SLOTS + s
            hit = jnp.max(jnp.where(match, 1.0, 0.0), axis=0, keepdims=True)
            coefs.append(jnp.sum(jnp.where(match, prob_rows, 0.0), axis=0, keepdims=True))
            hits = jnp.where(line == s, hit, hits)
        rank = jnp.dot(hits.astype(BF16), before, preferred_element_type=F32)
        own_rows = (r48 >= CAP) == (kk == 1)
        picks, scales = [], []
        for s in range(SLOTS):
            ok = own_rows & (hits[s : s + 1] > 0.5) & (rank[s : s + 1] == place)
            pick = jnp.where(ok, 1.0, 0.0)
            picks.append(pick)
            scales.append(jnp.sum(pick * coefs[s], axis=1, keepdims=True))
        pick = jnp.concatenate(picks, axis=0)
        scale_all += jnp.concatenate(scales, axis=0)
        sel_t[kk] = jnp.transpose(pick).astype(BF16)
        pick_all.append(pick.astype(BF16))

    def select(src, c):
        at = slice(c * CH, (c + 1) * CH)
        got = jnp.dot(pick_all[0], src[0, :, at], preferred_element_type=F32)
        return got + jnp.dot(pick_all[1], src[1, :, at], preferred_element_type=F32)

    class Route:
        def __init__(self, block, land, relay, sems, nth):
            ls, ys, yr, xs, xr, fs, fr = sems
            self.own = pltpu.make_async_copy(
                block(row_slots + side), land(q), ls.at[2 * nth]
            )
            self.own_far = pltpu.make_async_copy(
                relay(side), land(q_far), ls.at[2 * nth + 1]
            )
            self.y = [
                remote(block(far_slots + p), relay(p), ys.at[2 * nth + p], yr.at[2 * nth + p], far)
                for p in (0, 1)
            ]
            self.x_near, self.x_far = [], []
            for i in range(3):
                there, at = x_of[i] // 2, 6 * nth + i
                self.x_near.append(remote(block(row_slots + there), land(q),
                                          xs.at[at], xr.at[at], along[i]))
                self.x_far.append(remote(relay(there), land(q_far),
                                         xs.at[at + 3], xr.at[at + 3], along[i]))
            at = 8 * nth
            self.f_own = remote(block(row_slots + side), land(q), fs.at[at], fr.at[at], sib)
            self.f_far = remote(relay(side), land(q_far), fs.at[at + 1], fr.at[at + 1], sib)
            self.f_near_x, self.f_far_x = [], []
            for i in range(3):
                for kept, base, off in (
                    (self.f_near_x, yl * NX, 2), (self.f_far_x, (1 - yl) * NX, 5)
                ):
                    ref = land(base + x_from[i])
                    kept.append(remote(ref, ref, fs.at[at + off + i], fr.at[at + off + i], sib))

        def start_y(self):
            for cp in self.y:
                cp.start()

        def start_near(self):
            for cp in self.x_near:
                cp.start()
            self.own.start()
            self.f_own.start()

        def start_far(self):
            for cp in self.y:
                cp.wait_recv()
            for cp in self.x_far:
                cp.start()
            self.own_far.start()
            self.f_far.start()

        def arrive(self):
            for i in (1, 2, 0):
                self.x_near[i].wait_recv()
                self.f_near_x[i].start()
            for i in (1, 2, 0):
                self.x_far[i].wait_recv()
                self.f_far_x[i].start()
            for cp in [self.f_own, self.f_far] + self.f_near_x + self.f_far_x:
                cp.wait()
            self.own.wait()
            self.own_far.wait()

        def end(self):
            for cp in self.y + self.x_near + self.x_far:
                cp.wait_send()

    toks = Route(
        lambda s: snd_t.at[s], lambda c: xt.at[k, c], lambda p: rel_t.at[p],
        (tl, tys, tyr, txs, txr, tfs, tfr), 0,
    )
    chunk_of = [lax.rem(z + o, NC) for o in (0, 3, 1, 2)]

    def grad_route(n):
        c = chunk_of[n]
        return Route(
            lambda s: snd_g.at[c, s], lambda chip: xg.at[k, c, chip], lambda p: rel_g.at[n, p],
            (gl, gys, gyr, gxs, gxr, gfs, gfr), n,
        )

    grads = [grad_route(n) for n in range(NC)]

    local[2].wait()
    swap[2].wait()
    for c in range(NC):
        got = select(tokH, c)
        snd_t[:, :, c * CH : (c + 1) * CH] = got.astype(BF16).reshape(SLOTS, PAIR, CH)
    toks.start_y()
    toks.start_near()
    local[3].wait()
    swap[3].wait()
    for c in range(NC):
        got = select(grdH, c) * scale_all
        snd_g[c] = got.astype(BF16).reshape(SLOTS, PAIR, CH)
    toks.start_far()
    for r in grads:
        r.start_y()
    for n in range(NC):
        grads[n].start_near()
        grads[n].start_far()
    for cp in later:
        cp.wait()
    cand_copy.wait()

    toks.arrive()
    pre_gate = jnp.zeros((ROWS, HU), F32)
    pre_up = jnp.zeros((ROWS, HU), F32)
    for c in range(0, D, CH):
        rows = xt[c // HALF, :, :, c % HALF : c % HALF + CH].reshape(ROWS, CH)
        pre_gate += lax.dot_general(rows, wgv[:, c : c + CH], NT, preferred_element_type=F32)
        pre_up += lax.dot_general(rows, wuv[:, c : c + CH], NT, preferred_element_type=F32)
    sig = jax.nn.sigmoid(pre_gate)
    act = pre_gate * sig
    hid_t[...] = jnp.transpose(act * pre_up).astype(BF16)

    def grad_share(zd, yd):
        at = pl.ds(pl.multiple_of(yd * SHARE, SHARE), SHARE)
        rows = xg[zd // NC, lax.rem(zd, NC), :, :, at].reshape(ROWS, SHARE)
        return jnp.dot(hid_t[...], rows, preferred_element_type=F32).astype(BF16)

    y_copies = [
        remote(wy_snd.at[n], wy_rcv.at[n], s_y.at[n], r_y.at[n], ypart) for n in range(NZ)
    ]

    def shares(pair):
        for n in pair:
            wy_snd[n] = grad_share(lax.rem(z + n, NZ), 1 - yh)
            y_copies[n].start()
        for n in pair:
            w_own[n] = grad_share(lax.rem(z + n, NZ), yh)

    cand_a = mine[0:1, 0:1]
    cand_b = theirs[0:1, 0:1]

    def term(n, c):
        a, b = w_own[n].astype(F32), wy_rcv[n].astype(F32)
        return jnp.where(cand_a == c, a, 0.0) + jnp.where(cand_b == c, b, 0.0)

    def hops(snd, rcv, ssem, rsem, count, to):
        return [
            [
                remote(snd.at[t, c], rcv.at[t, c], ssem.at[2 * t + c], rsem.at[2 * t + c], to)
                for c in (0, 1)
            ]
            for t in range(count)
        ]

    downs = hops(rm_snd, rm_rcv, s_m, r_m, 4, zdn)
    ups = hops(rp_snd, rp_rcv, s_q, r_q, 3, zup)

    def ring(ring_hops, snd, rcv, t, n):
        y_copies[n].wait_recv()
        for c in (0, 1):
            value = term(n, c)
            if t > 0:
                ring_hops[t - 1][c].wait_recv()
                value = value + rcv[t - 1, c].astype(F32)
            snd[t, c] = value.astype(BF16)
            ring_hops[t][c].start()

    down = lambda t: ring(downs, rm_snd, rm_rcv, t, 4 + t)
    up = lambda t: ring(ups, rp_snd, rp_rcv, t, 3 - t)

    grads[0].arrive()
    shares((4, 0))
    grads[1].arrive()
    shares((3, 7))
    down(0)
    grads[2].arrive()
    shares((5, 1))
    up(0)
    grads[3].arrive()
    shares((6, 2))
    down(1)

    d_hidden = jnp.zeros((ROWS, HU), F32)
    for c in range(D // CH):
        rows = xg[c // NC, c % NC].reshape(ROWS, CH)
        d_hidden += lax.dot_general(
            rows, wdv[:, c * CH : (c + 1) * CH], NT, preferred_element_type=F32
        )
    dgv[...] = (d_hidden * pre_up * sig * (1.0 + pre_gate * (1.0 - sig))).astype(BF16)
    duv[...] = (d_hidden * act).astype(BF16)
    up(1)
    down(2)

    def partial(start):
        at = pl.ds(pl.multiple_of(start, CH), CH)
        got = jnp.dot(dgv[...], wgv[:, at], preferred_element_type=F32)
        return got + jnp.dot(duv[...], wuv[:, at], preferred_element_type=F32)

    for c in range(0, HALF, CH):
        got = partial((1 - k) * HALF + c)
        p_snd[:, :, c : c + CH] = got.astype(BF16).reshape(CHIPS, PAIR, CH)
    p_copy = remote(p_snd, p_rcv, s_p.at[0], r_p.at[0], sib)
    p_copy.start()
    up(2)
    down(3)
    for c in range(0, HALF, CH):
        p_own[:, :, c : c + CH] = partial(k * HALF + c).reshape(CHIPS, PAIR, CH)
    p_copy.wait()

    def both_cores(chip):
        return (p_own[chip] + p_rcv[chip].astype(F32)).astype(BF16)

    r_copies = []
    for i in range(3):
        for j, (base, dst) in enumerate((((1 - yl) * NX, relr), (yl * NX, fin))):
            at = 2 * i + j
            r_snd[at] = both_cores(base + x_of[i])
            cp = remote(r_snd.at[at], dst.at[x], s_r.at[at], r_r.at[at], along[i])
            cp.start()
            r_copies.append(cp)
    relr[x] = both_cores(q_far)
    fin[x] = both_cores(q)

    y_copies[0].wait_recv()
    total = [term(0, c) for c in (0, 1)]
    for c in (0, 1):
        ups[-1][c].wait_recv()
        downs[-1][c].wait_recv()
        grad = total[c] + rp_rcv[2, c].astype(F32) + rm_rcv[3, c].astype(F32)
        first = beta_one * m1v[c] + (1.0 - beta_one) * grad
        second = beta_two * m2v[c] + (1.0 - beta_two) * grad * grad
        nf_out[c] = first
        ns_out[c] = second
        step = first / first_fix / (jnp.sqrt(second / second_fix) + adam_eps)
        dall[z, c] = step.astype(BF16)

    d_copies = []

    def use(n, zo):
        at = cols(zo * 2 + yh)
        first, second = dall[zo, 0].astype(F32), dall[zo, 1].astype(F32)
        dy[n] = jnp.where(cand_b == 0, first, second).astype(BF16)
        cp = remote(dy.at[n], sd_out.at[0, :, at], s_d.at[n], r_d.at[n], ypart)
        cp.start()
        d_copies.append(cp)
        sd_out[0, :, at] = jnp.where(cand_a == 0, first, second).astype(BF16)

    def passes(zo, ssem, rsem, t, to):
        return [
            remote(dall.at[zo, c], dall.at[zo, c], ssem.at[2 * t + c], rsem.at[2 * t + c], to)
            for c in (0, 1)
        ]

    below = [lax.rem(z + NZ - t, NZ) for t in range(5)]
    above = [lax.rem(z + t, NZ) for t in range(4)]
    a_up = [passes(below[t], s_ap, r_ap, t, zup) for t in range(4)]
    a_dn = [passes(above[t], s_am, r_am, t, zdn) for t in range(3)]
    for c in (0, 1):
        a_up[0][c].start()
        a_dn[0][c].start()
    use(0, z)

    def relay_back():
        for cp in r_copies:
            cp.wait_recv()
        sent = []
        for p in (0, 1):
            got = relr[2 * p].astype(F32) + relr[2 * p + 1].astype(F32)
            rel_s[p] = got.astype(BF16)
            cp = remote(rel_s.at[p], rback.at[row_slots + p], s_ry.at[p], r_ry.at[p], far)
            cp.start()
            sent.append(cp)
        for p in (0, 1):
            got = fin[2 * p].astype(F32) + fin[2 * p + 1].astype(F32)
            rback[row_slots + p] = got.astype(BF16)
        return sent

    def combine():
        for cp in far_copies:
            cp.wait_recv()
        for c in range(0, HALF, CH):
            rows = rback[:, :, c : c + CH].reshape(SLOTS * PAIR, CH)
            for kk in (0, 1):
                got = jnp.dot(sel_t[kk], rows, preferred_element_type=F32)
                tgv[kk, :, c : c + CH] = got.astype(BF16)
        across = remote(tgv.at[1 - k], tg_out.at[:, mine_cols], s_tg.at[0], r_tg.at[0], sib)
        across.start()
        tg_out[:, mine_cols] = tgv[k]
        return across

    for t in range(4):
        for c in (0, 1):
            a_up[t][c].wait_recv()
            if t < 3:
                a_up[t + 1][c].start()
            if t < 3:
                a_dn[t][c].wait_recv()
                if t < 2:
                    a_dn[t + 1][c].start()
        use(1 + t, below[t + 1])
        if t < 3:
            use(5 + t, above[t + 1])
        if t == 1:
            far_copies = relay_back()
        if t == 2:
            tg_copy = combine()

    tg_copy.wait()
    for cp in d_copies:
        cp.wait()
    for r in [toks] + grads:
        r.end()
    for cp in y_copies + r_copies + far_copies:
        cp.wait_send()
    for hop in downs + ups + a_up + a_dn:
        for cp in hop:
            cp.wait_send()


def step(tokens, expert_ids, gate_probs, placement, gate_weight, up_weight, down_weight,
         out_grad, moment_first, moment_second):
    def vm(*shape, dtype=BF16):
        return pltpu.VMEM(shape, dtype)

    dma = lambda n: pltpu.SemaphoreType.DMA((n,))
    anywhere = pl.BlockSpec(memory_space=pl.ANY)
    outs = pl.pallas_call(
        body,
        out_shape=(
            vm(TOK, D), vm(1, HU, D), vm(2, HU, SHARE, dtype=F32), vm(2, HU, SHARE, dtype=F32),
        ),
        in_specs=[anywhere] * 3 + [pl.BlockSpec(memory_space=pltpu.SMEM)] + [anywhere] * 6,
        out_specs=(pl.BlockSpec(memory_space=pltpu.VMEM),) * 4,
        scratch_shapes=[
            vm(2, TOK, HALF), vm(2, TOK, HALF),
            vm(2, 8, TOK, dtype=jnp.int32), vm(2, 8, TOK, dtype=F32),
            vm(2, TOK, SLOTS * PAIR),
            vm(SLOTS, PAIR, HALF), vm(NC, SLOTS, PAIR, CH),
            vm(2, PAIR, HALF), vm(NC, 2, PAIR, CH),
            vm(2, CHIPS, PAIR, HALF), vm(2, NC, CHIPS, PAIR, CH),
            vm(HU, D), vm(HU, D), vm(HU, D),
            vm(2, HU, SHARE, dtype=F32), vm(2, HU, SHARE, dtype=F32),
            vm(HU, ROWS), vm(ROWS, HU), vm(ROWS, HU),
            vm(CHIPS, PAIR, HALF), vm(CHIPS, PAIR, HALF), vm(CHIPS, PAIR, HALF, dtype=F32),
            vm(6, PAIR, HALF), vm(NX, PAIR, HALF), vm(NX, PAIR, HALF),
            vm(2, PAIR, HALF), vm(SLOTS, PAIR, HALF), vm(2, TOK, HALF),
            vm(8, 128, dtype=jnp.int32), vm(8, 128, dtype=jnp.int32),
            vm(NZ, HU, SHARE), vm(NZ, HU, SHARE), vm(NZ, HU, SHARE),
            vm(4, 2, HU, SHARE), vm(4, 2, HU, SHARE), vm(3, 2, HU, SHARE), vm(3, 2, HU, SHARE),
            vm(NZ, 2, HU, SHARE), vm(NZ, HU, SHARE),
            dma(9), dma(4), dma(4),
            dma(2), dma(2), dma(2), dma(6), dma(6), dma(8), dma(8),
            dma(2 * NC), dma(2 * NC), dma(2 * NC), dma(6 * NC), dma(6 * NC), dma(8 * NC),
            dma(8 * NC),
            dma(1), dma(1), dma(6), dma(6), dma(2), dma(2), dma(1), dma(1),
            dma(1), dma(1), dma(8), dma(8), dma(8), dma(8), dma(6), dma(6),
            dma(6), dma(6), dma(8), dma(8), dma(8), dma(8),
        ],
        compiler_params=pltpu.CompilerParams(
            collective_id=0, has_side_effects=True, vmem_limit_bytes=60 * 2**20
        ),
    )(tokens, expert_ids.T, gate_probs.T, placement, jnp.swapaxes(gate_weight, 1, 2),
      jnp.swapaxes(up_weight, 1, 2), down_weight, out_grad, moment_first, moment_second)
    return outs


def solution(mesh):
    return jax.shard_map(
        step,
        mesh=mesh,
        in_specs=(
            P(("grp", "ep"), None),
            P(("grp", "ep"), None),
            P(("grp", "ep"), None),
            P("grp", None),
            P("grp", None, "ep"),
            P("grp", None, "ep"),
            P("grp", "ep", None),
            P(("grp", "ep"), None),
            P(None, "ep", "grp"),
            P(None, "ep", "grp"),
        ),
        out_specs=(
            P(("grp", "ep"), None),
            P("grp", "ep", None),
            P(None, "ep", "grp"),
            P(None, "ep", "grp"),
        ),
        check_vma=False,
    )
```

time: 138 us -> 110 us (0.80)
  the two profiles are of different devices: /device:TPU:56 before, /device:TPU:8 now
where the time goes in v2:
time: 110 us
  Pallas kernels  106 us (96%)
  local copies, waits for them, and re-layouts  3.78 us (3%)
    pallas_call x1, Pallas kernels, step(): pl.pallas_call(body, out_shape=(vm(TOK, D), vm(1, HU, D), vm(2, HU, SHARE...  106 us
    unnamed x4, local copies, waits for them, and re-layouts  3.78 us

profile of v2, /device:TPU:8, one launch (start us, length us, event | category | flops | bytes accessed | tf_op | source)
XLA Modules:
  0.0 110.2 jit_solution(8903649102088109562)
XLA Ops:
  0.6 105.7 %shard_map.129 = (bf16[192,4096]{1,0:T(8,128)(2,1)S(1)}, bf16[1,192,4096]{2,1,0:T(8,128)(2,1)S(1)}, f32[2,192,256]{2,1,0:T(8,128)S(1)}, f32[2,192,256]{2,1,0:T(8,128)S(1)}) custom-call(bf16[192,4096]{1,0:T(8,128)(2,1)} %tok.1, s32[8,192]{1,0:T(8,128)} %bitcast.6, f32[8,192]{1,0:T(8,128)} %bitcast.7, s32[1,4]{1,0:T(1,128)} %plc.1, ...), custom_call_target="tpu_custom_call" | custom-call | tf_op jit(solution)/shard_map/pallas_call | solution.py:473
  106.4 1.1 %copy.18 = bf16[192,4096]{1,0:T(8,128)(2,1)} copy(bf16[192,4096]{1,0:T(8,128)(2,1)S(1)} %get-tuple-element.4) | data formatting | bytes 3145728
  107.5 0.7 copy.20
  108.3 0.7 copy.21
  109.0 1.1 %copy.19 = bf16[1,192,4096]{2,1,0:T(8,128)(2,1)} copy(bf16[1,192,4096]{2,1,0:T(8,128)(2,1)S(1)} %get-tuple-element.5) | data formatting | bytes 3145728

commit v3 on v2

v3 whole, which is shorter than its diff:
```python
import math

import jax
import jax.numpy as jnp
from jax import lax
from jax.experimental import pallas as pl
from jax.experimental.pallas import tpu as pltpu
from jax.sharding import PartitionSpec as P

MESH = pl.DeviceIdType.MESH
F32 = jnp.float32
BF16 = jnp.bfloat16

D = 4096
HALF = 2048
TOK = 192
HU = 192
CAP = 24
PAIR = 2 * CAP
SLOTS = 4
CHIPS = 8
NX = 4
NZ = 8
SHARE = 256
ROWS = CHIPS * PAIR
CH = 512

beta_one = 0.9
beta_two = 0.999
adam_eps = 1e-08
first_fix = 1.0 - math.exp(1000.0 * math.log(0.9))
second_fix = 1.0 - math.exp(1000.0 * math.log(0.999))

XD = (2, 1, 3)
NC = 4
NR = 2
PIECE = HU // NR
CHUNKS = ((4, 0), (3, 5), (2, 6), (1, 7))
NT = (((1,), (1,)), ((), ()))


def body(
    tok, ids, prb, plc, wg, wu, wd, og, m1, m2,
    tg_out, sd_out, nf_out, ns_out,
    tokH, grdH, idsH, prbH, sel_t, snd_t, snd_g, rel_t, rel_g, xt, xg,
    wgv, wuv, wdv, m1v, m2v, hid_t, dhv, dgv, duv,
    p_snd, p_rcv, p_own, r_snd, fin, relr, rel_s, rback, tgv,
    mine, theirs, wy_snd, wy_rcv, w_own,
    rm_snd, rm_rcv, rp_snd, rp_rcv, dall, dy,
    lsem, s_in, r_in,
    tl, tys, tyr, txs, txr, tfs, tfr, gl, gys, gyr, gxs, gxr, gfs, gfr,
    s_p, r_p, s_r, r_r, s_ry, r_ry, s_tg, r_tg,
    s_c, r_c, s_y, r_y, s_m, r_m, s_q, r_q, s_am, r_am, s_ap, r_ap, s_d, r_d,
):
    g = lax.axis_index("grp")
    e = lax.axis_index("ep")
    z, yh = g // 2, lax.rem(g, 2)
    q, k = e // 2, lax.rem(e, 2)
    yl, x = q // NX, lax.rem(q, NX)
    slot = q // 2
    row_slots, far_slots = yl * 2, (1 - yl) * 2
    side = x // 2
    q_far = (1 - yl) * NX + x
    sib = {"grp": g, "ep": q * 2 + 1 - k}
    far = {"grp": g, "ep": q_far * 2 + k}
    ypart = {"grp": z * 2 + 1 - yh, "ep": e}
    zup = {"grp": lax.rem(z + 1, NZ) * 2 + yh, "ep": e}
    zdn = {"grp": lax.rem(z + NZ - 1, NZ) * 2 + yh, "ep": e}
    x_of = [lax.rem(x + d, NX) for d in XD]
    x_from = [lax.rem(x - d + NX, NX) for d in XD]
    along = [{"grp": g, "ep": (yl * NX + xd) * 2 + k} for xd in x_of]

    def remote(src, dst, ssem, rsem, to):
        return pltpu.make_async_remote_copy(
            src_ref=src, dst_ref=dst, send_sem=ssem, recv_sem=rsem, device_id=to,
            device_id_type=MESH,
        )

    def cols(i):
        return pl.ds(pl.multiple_of(i * SHARE, SHARE), SHARE)

    mine_cols = pl.ds(pl.multiple_of(k * HALF, HALF), HALF)
    other_cols = pl.ds(pl.multiple_of((1 - k) * HALF, HALF), HALF)

    local = [
        pltpu.make_async_copy(ids, idsH.at[k], lsem.at[0]),
        pltpu.make_async_copy(prb, prbH.at[k], lsem.at[1]),
        pltpu.make_async_copy(tok.at[:, mine_cols], tokH.at[k], lsem.at[2]),
    ]
    local_g = [
        pltpu.make_async_copy(og.at[:, cols(2 * i + k)], grdH.at[k, i], lsem.at[8 + i])
        for i in range(NZ)
    ]
    later = [
        pltpu.make_async_copy(wg.at[0], wgv, lsem.at[3]),
        pltpu.make_async_copy(wu.at[0], wuv, lsem.at[4]),
        pltpu.make_async_copy(wd.at[0], wdv, lsem.at[5]),
        pltpu.make_async_copy(m1, m1v, lsem.at[6]),
        pltpu.make_async_copy(m2, m2v, lsem.at[7]),
    ]
    for cp in local + local_g:
        cp.start()
    mine[...] = jnp.zeros((8, 128), jnp.int32) + plc[0, slot]

    barrier = pltpu.get_barrier_semaphore()
    greet = [sib, far, ypart, zup, zdn] + along
    for to in greet:
        pl.semaphore_signal(barrier, inc=1, device_id=to, device_id_type=MESH)
    pl.semaphore_wait(barrier, len(greet))

    swap = [
        remote(ids, idsH.at[k], s_in.at[0], r_in.at[0], sib),
        remote(prb, prbH.at[k], s_in.at[1], r_in.at[1], sib),
        remote(tok.at[:, other_cols], tokH.at[k], s_in.at[2], r_in.at[2], sib),
    ]
    swap_g = [
        remote(og.at[:, cols(2 * i + 1 - k)], grdH.at[k, i], s_in.at[3 + i], r_in.at[3 + i], sib)
        for i in range(NZ)
    ]
    for cp in swap + swap_g:
        cp.start()
    cand_copy = remote(mine, theirs, s_c.at[0], r_c.at[0], ypart)
    cand_copy.start()
    for cp in later:
        cp.start()

    for i in (0, 1):
        local[i].wait()
        swap[i].wait()
    row = lax.broadcasted_iota(jnp.int32, (TOK, TOK), 0)
    col = lax.broadcasted_iota(jnp.int32, (TOK, TOK), 1)
    before = jnp.where(row < col, 1.0, 0.0).astype(BF16)
    line = lax.broadcasted_iota(jnp.int32, (8, TOK), 0)
    r48 = lax.broadcasted_iota(jnp.int32, (PAIR, TOK), 0)
    place = jnp.where(r48 >= CAP, r48 - CAP, r48).astype(F32)
    pick_all = []
    scale_all = jnp.zeros((SLOTS * PAIR, 1), F32)
    for kk in (0, 1):
        id_rows, prob_rows = idsH[kk], prbH[kk]
        hits = jnp.zeros((8, TOK), F32)
        coefs = []
        for s in range(SLOTS):
            match = id_rows == plc[0, s] * SLOTS + s
            hit = jnp.max(jnp.where(match, 1.0, 0.0), axis=0, keepdims=True)
            coefs.append(jnp.sum(jnp.where(match, prob_rows, 0.0), axis=0, keepdims=True))
            hits = jnp.where(line == s, hit, hits)
        rank = jnp.dot(hits.astype(BF16), before, preferred_element_type=F32)
        own_rows = (r48 >= CAP) == (kk == 1)
        picks, scales = [], []
        for s in range(SLOTS):
            ok = own_rows & (hits[s : s + 1] > 0.5) & (rank[s : s + 1] == place)
            pick = jnp.where(ok, 1.0, 0.0)
            picks.append(pick)
            scales.append(jnp.sum(pick * coefs[s], axis=1, keepdims=True))
        pick = jnp.concatenate(picks, axis=0)
        scale_all += jnp.concatenate(scales, axis=0)
        sel_t[kk] = jnp.transpose(pick).astype(BF16)
        pick_all.append(pick.astype(BF16))

    def select(rows_a, rows_b):
        got = jnp.dot(pick_all[0], rows_a, preferred_element_type=F32)
        return got + jnp.dot(pick_all[1], rows_b, preferred_element_type=F32)

    class Route:
        def __init__(self, block, land, relay, sems, nth):
            ls, ys, yr, xs, xr, fs, fr = sems
            self.own = pltpu.make_async_copy(
                block(row_slots + side), land(q), ls.at[2 * nth]
            )
            self.own_far = pltpu.make_async_copy(
                relay(side), land(q_far), ls.at[2 * nth + 1]
            )
            self.y = [
                remote(block(far_slots + p), relay(p), ys.at[2 * nth + p], yr.at[2 * nth + p], far)
                for p in (0, 1)
            ]
            self.x_near, self.x_far = [], []
            for i in range(3):
                there, at = x_of[i] // 2, 6 * nth + i
                self.x_near.append(remote(block(row_slots + there), land(q),
                                          xs.at[at], xr.at[at], along[i]))
                self.x_far.append(remote(relay(there), land(q_far),
                                         xs.at[at + 3], xr.at[at + 3], along[i]))
            at = 8 * nth
            self.f_own = remote(block(row_slots + side), land(q), fs.at[at], fr.at[at], sib)
            self.f_far = remote(relay(side), land(q_far), fs.at[at + 1], fr.at[at + 1], sib)
            self.f_near_x, self.f_far_x = [], []
            for i in range(3):
                for kept, base, off in (
                    (self.f_near_x, yl * NX, 2), (self.f_far_x, (1 - yl) * NX, 5)
                ):
                    ref = land(base + x_from[i])
                    kept.append(remote(ref, ref, fs.at[at + off + i], fr.at[at + off + i], sib))

        def start_y(self):
            for cp in self.y:
                cp.start()

        def start_near(self):
            for cp in self.x_near:
                cp.start()
            self.own.start()
            self.f_own.start()

        def start_far(self):
            for cp in self.y:
                cp.wait_recv()
            for cp in self.x_far:
                cp.start()
            self.own_far.start()
            self.f_far.start()

        def arrive(self):
            for i in (1, 2, 0):
                self.x_near[i].wait_recv()
                self.f_near_x[i].start()
            for i in (1, 2, 0):
                self.x_far[i].wait_recv()
                self.f_far_x[i].start()
            for cp in [self.f_own, self.f_far] + self.f_near_x + self.f_far_x:
                cp.wait()
            self.own.wait()
            self.own_far.wait()

        def end(self):
            for cp in self.y + self.x_near + self.x_far:
                cp.wait_send()

    toks = Route(
        lambda s: snd_t.at[s], lambda c: xt.at[k, c], lambda p: rel_t.at[p],
        (tl, tys, tyr, txs, txr, tfs, tfr), 0,
    )
    owner = [lax.rem(z + n, NZ) for n in range(NZ)]

    def grad_route(n):
        return Route(
            lambda s: snd_g.at[n, s], lambda chip: xg.at[k, n, chip], lambda p: rel_g.at[n, p],
            (gl, gys, gyr, gxs, gxr, gfs, gfr), n,
        )

    grads = [grad_route(n) for n in range(NC)]

    local[2].wait()
    swap[2].wait()
    for c in range(NC):
        at = slice(c * CH, (c + 1) * CH)
        got = select(tokH[0, :, at], tokH[1, :, at])
        snd_t[:, :, at] = got.astype(BF16).reshape(SLOTS, PAIR, CH)
    toks.start_y()
    toks.start_near()
    for cp in local_g + swap_g:
        cp.wait()
    for c, pair in enumerate(CHUNKS):
        for j, n in enumerate(pair):
            got = select(grdH[0, owner[n]], grdH[1, owner[n]]) * scale_all
            at = slice(j * SHARE, (j + 1) * SHARE)
            snd_g[c, :, :, at] = got.astype(BF16).reshape(SLOTS, PAIR, SHARE)
    for r in grads:
        r.start_y()
    grads[0].start_near()
    toks.start_far()
    grads[0].start_far()
    for n in range(1, NC):
        grads[n].start_near()
        grads[n].start_far()
    for cp in later:
        cp.wait()
    cand_copy.wait()

    toks.arrive()
    pre_gate = jnp.zeros((ROWS, HU), F32)
    pre_up = jnp.zeros((ROWS, HU), F32)
    for c in range(0, D, CH):
        rows = xt[c // HALF, :, :, c % HALF : c % HALF + CH].reshape(ROWS, CH)
        pre_gate += lax.dot_general(rows, wgv[:, c : c + CH], NT, preferred_element_type=F32)
        pre_up += lax.dot_general(rows, wuv[:, c : c + CH], NT, preferred_element_type=F32)
    sig = jax.nn.sigmoid(pre_gate)
    act = pre_gate * sig
    hid_t[...] = jnp.transpose(act * pre_up).astype(BF16)

    def rows_of(n, yd):
        [(c, j)] = [(c, pair.index(n)) for c, pair in enumerate(CHUNKS) if n in pair]
        return xg[yd, c, :, :, j * SHARE : (j + 1) * SHARE].reshape(ROWS, SHARE)

    def grad_share(n, yd):
        got = jnp.dot(hid_t[...], rows_of(n, yd), preferred_element_type=F32)
        return got.astype(BF16).reshape(NR, PIECE, SHARE)

    def pieces(n, make):
        return [make(n, r, NR * n + r) for r in range(NR)]

    y_copies = [
        pieces(n, lambda n, r, i: remote(wy_snd.at[n, r], wy_rcv.at[n, r], s_y.at[i], r_y.at[i],
                                         ypart))
        for n in range(NZ)
    ]

    def shares(pair):
        for n in pair:
            wy_snd[n] = grad_share(n, 1 - yh)
            for cp in y_copies[n]:
                cp.start()
        for n in pair:
            w_own[n] = grad_share(n, yh)

    cand_a = mine[0:1, 0:1]
    cand_b = theirs[0:1, 0:1]

    def term(n, r):
        y_copies[n][r].wait_recv()
        a, b = w_own[n, r].astype(F32), wy_rcv[n, r].astype(F32)
        return [
            jnp.where(cand_a == c, a, 0.0) + jnp.where(cand_b == c, b, 0.0) for c in (0, 1)
        ]

    def hops(snd, rcv, ssem, rsem, to):
        return [
            pieces(t, lambda t, r, i: remote(snd.at[t, r], rcv.at[t, r], ssem.at[i], rsem.at[i], to))
            for t in range(4)
        ]

    downs = hops(rm_snd, rm_rcv, s_m, r_m, zdn)
    ups = hops(rp_snd, rp_rcv, s_q, r_q, zup)

    def ring(ring_hops, snd, rcv, t, n, first):
        for r in range(NR):
            if t == 0 and r != first:
                continue
            values = term(n, r)
            more = t > 1 or (t == 1 and r == first)
            if more:
                ring_hops[t - 1][r].wait_recv()
            for c in (0, 1):
                value = values[c]
                if more:
                    value = value + rcv[t - 1, r, c].astype(F32)
                snd[t, r, c] = value.astype(BF16)
            ring_hops[t][r].start()

    def down(t):
        ring(downs, rm_snd, rm_rcv, t, 4 + t, 0)

    def up(t):
        ring(ups, rp_snd, rp_rcv, t, 4 - t, 1)

    def d_hidden(c):
        got = None
        for n in CHUNKS[c]:
            for yd in (0, 1):
                at = cols(owner[n] * 2 + yd)
                part = lax.dot_general(rows_of(n, yd), wdv[:, at], NT, preferred_element_type=F32)
                got = part if got is None else got + part
        if c == 0:
            dhv[...] = got
        else:
            dhv[...] += got

    grads[0].arrive()
    shares(CHUNKS[0])
    d_hidden(0)
    grads[1].arrive()
    shares(CHUNKS[1])
    down(0)
    up(0)
    d_hidden(1)
    grads[2].arrive()
    shares(CHUNKS[2])
    up(1)
    down(1)
    d_hidden(2)
    grads[3].arrive()
    shares(CHUNKS[3])
    d_hidden(3)
    d_hid = dhv[...]
    dgv[...] = (d_hid * pre_up * sig * (1.0 + pre_gate * (1.0 - sig))).astype(BF16)
    duv[...] = (d_hid * act).astype(BF16)
    up(2)
    down(2)

    def partial(start):
        at = pl.ds(pl.multiple_of(start, CH), CH)
        got = jnp.dot(dgv[...], wgv[:, at], preferred_element_type=F32)
        return got + jnp.dot(duv[...], wuv[:, at], preferred_element_type=F32)

    p_copies = [
        remote(p_snd.at[c], p_rcv.at[c], s_p.at[c], r_p.at[c], sib) for c in range(NC)
    ]
    for c in range(NC):
        got = partial((1 - k) * HALF + c * CH)
        p_snd[c] = got.astype(BF16).reshape(CHIPS, PAIR, CH)
        p_copies[c].start()
    for c in range(NC):
        p_own[c] = partial(k * HALF + c * CH).reshape(CHIPS, PAIR, CH)

    r_copies = []

    def send_back(c):
        def both_cores(chip):
            return (p_own[c, chip] + p_rcv[c, chip].astype(F32)).astype(BF16)

        p_copies[c].wait()
        sent = []
        for i in range(3):
            for j, (base, dst) in enumerate((((1 - yl) * NX, relr), (yl * NX, fin))):
                at = 2 * i + j
                r_snd[c, at] = both_cores(base + x_of[i])
                cp = remote(r_snd.at[c, at], dst.at[c, x],
                            s_r.at[6 * c + at], r_r.at[6 * c + at], along[i])
                cp.start()
                sent.append(cp)
        relr[c, x] = both_cores(q_far)
        fin[c, x] = both_cores(q)
        r_copies.append(sent)

    up(3)
    down(3)
    for c in range(NC):
        send_back(c)

    d_copies = []

    def use(n, zo, r):
        at, rows = cols(zo * 2 + yh), slice(r * PIECE, (r + 1) * PIECE)
        first, second = dall[zo, r, 0].astype(F32), dall[zo, r, 1].astype(F32)
        dy[n, r] = jnp.where(cand_b == 0, first, second).astype(BF16)
        i = NR * n + r
        cp = remote(dy.at[n, r], sd_out.at[0, rows, at], s_d.at[i], r_d.at[i], ypart)
        cp.start()
        d_copies.append(cp)
        sd_out[0, rows, at] = jnp.where(cand_a == 0, first, second).astype(BF16)

    below = [lax.rem(z + NZ - t, NZ) for t in range(5)]
    above = [lax.rem(z + t, NZ) for t in range(5)]

    def passes(zo, ssem, rsem, t, to):
        return pieces(t, lambda t, r, i: remote(dall.at[zo, r], dall.at[zo, r], ssem.at[i],
                                                rsem.at[i], to))

    a_up = [passes(below[t], s_ap, r_ap, t, zup) for t in range(4)]
    a_dn = [passes(above[t], s_am, r_am, t, zdn) for t in range(4)]

    for r in range(NR):
        rows = slice(r * PIECE, (r + 1) * PIECE)
        grads_r = term(0, r)
        ups[3][r].wait_recv()
        downs[3][r].wait_recv()
        for c in (0, 1):
            grad = grads_r[c] + rp_rcv[3, r, c].astype(F32) + rm_rcv[3, r, c].astype(F32)
            first = beta_one * m1v[c, rows] + (1.0 - beta_one) * grad
            second = beta_two * m2v[c, rows] + (1.0 - beta_two) * grad * grad
            nf_out[c, rows] = first
            ns_out[c, rows] = second
            step = first / first_fix / (jnp.sqrt(second / second_fix) + adam_eps)
            dall[z, r, c] = step.astype(BF16)
        a_up[0][r].start()
        a_dn[0][r].start()
        use(0, z, r)

    far_copies = []

    def relay_back(c):
        for cp in r_copies[c]:
            cp.wait_recv()
        for p in (0, 1):
            got = relr[c, 2 * p].astype(F32) + relr[c, 2 * p + 1].astype(F32)
            rel_s[c, p] = got.astype(BF16)
            at = 2 * c + p
            cp = remote(rel_s.at[c, p], rback.at[c, row_slots + p], s_ry.at[at], r_ry.at[at], far)
            cp.start()
            far_copies.append(cp)
        for p in (0, 1):
            got = fin[c, 2 * p].astype(F32) + fin[c, 2 * p + 1].astype(F32)
            rback[c, row_slots + p] = got.astype(BF16)

    tg_copies = []

    def combine(c):
        for cp in far_copies[2 * c : 2 * c + 2]:
            cp.wait_recv()
        rows = rback[c].reshape(SLOTS * PAIR, CH)
        for kk in (0, 1):
            got = jnp.dot(sel_t[kk], rows, preferred_element_type=F32)
            tgv[c, kk] = got.astype(BF16)
        at = pl.ds(pl.multiple_of(k * HALF + c * CH, CH), CH)
        cp = remote(tgv.at[c, 1 - k], tg_out.at[:, at], s_tg.at[c], r_tg.at[c], sib)
        cp.start()
        tg_copies.append(cp)
        tg_out[:, at] = tgv[c, k]

    for t in range(4):
        for r in range(NR):
            if t < 3 or r == 0:
                a_up[t][r].wait_recv()
                if t < 2 or (t == 2 and r == 0):
                    a_up[t + 1][r].start()
                use(1 + t, below[t + 1], r)
            if t < 3 or r == 1:
                a_dn[t][r].wait_recv()
                if t < 2 or (t == 2 and r == 1):
                    a_dn[t + 1][r].start()
                use(5 + t if t < 3 else 4, above[t + 1], r)
        if t == 0:
            relay_back(0)
            relay_back(1)
        if t == 1:
            relay_back(2)
            relay_back(3)
            combine(0)
        if t == 2:
            combine(1)
            combine(2)
    combine(3)

    for cp in tg_copies + d_copies:
        cp.wait()
    for r in [toks] + grads:
        r.end()
    for cp in far_copies:
        cp.wait_send()
    for sent in r_copies + y_copies:
        for cp in sent:
            cp.wait_send()
    for t in range(4):
        for c in (0, 1):
            if t > 0 or c == 0:
                downs[t][c].wait_send()
            if t > 0 or c == 1:
                ups[t][c].wait_send()
            if t < 3 or c == 0:
                a_up[t][c].wait_send()
            if t < 3 or c == 1:
                a_dn[t][c].wait_send()


def step(tokens, expert_ids, gate_probs, placement, gate_weight, up_weight, down_weight,
         out_grad, moment_first, moment_second):
    def vm(*shape, dtype=BF16):
        return pltpu.VMEM(shape, dtype)

    dma = lambda n: pltpu.SemaphoreType.DMA((n,))
    anywhere = pl.BlockSpec(memory_space=pl.ANY)
    outs = pl.pallas_call(
        body,
        out_shape=(
            vm(TOK, D), vm(1, HU, D), vm(2, HU, SHARE, dtype=F32), vm(2, HU, SHARE, dtype=F32),
        ),
        in_specs=[anywhere] * 3 + [pl.BlockSpec(memory_space=pltpu.SMEM)] + [anywhere] * 6,
        out_specs=(pl.BlockSpec(memory_space=pltpu.VMEM),) * 4,
        scratch_shapes=[
            vm(2, TOK, HALF), vm(2, NZ, TOK, SHARE),
            vm(2, 8, TOK, dtype=jnp.int32), vm(2, 8, TOK, dtype=F32),
            vm(2, TOK, SLOTS * PAIR),
            vm(SLOTS, PAIR, HALF), vm(NC, SLOTS, PAIR, CH),
            vm(2, PAIR, HALF), vm(NC, 2, PAIR, CH),
            vm(2, CHIPS, PAIR, HALF), vm(2, NC, CHIPS, PAIR, CH),
            vm(HU, D), vm(HU, D), vm(HU, D),
            vm(2, HU, SHARE, dtype=F32), vm(2, HU, SHARE, dtype=F32),
            vm(HU, ROWS), vm(ROWS, HU, dtype=F32), vm(ROWS, HU), vm(ROWS, HU),
            vm(NC, CHIPS, PAIR, CH), vm(NC, CHIPS, PAIR, CH),
            vm(NC, CHIPS, PAIR, CH, dtype=F32),
            vm(NC, 6, PAIR, CH), vm(NC, NX, PAIR, CH), vm(NC, NX, PAIR, CH),
            vm(NC, 2, PAIR, CH), vm(NC, SLOTS, PAIR, CH), vm(NC, 2, TOK, CH),
            vm(8, 128, dtype=jnp.int32), vm(8, 128, dtype=jnp.int32),
            vm(NZ, NR, PIECE, SHARE), vm(NZ, NR, PIECE, SHARE), vm(NZ, NR, PIECE, SHARE),
            vm(4, NR, 2, PIECE, SHARE), vm(4, NR, 2, PIECE, SHARE),
            vm(4, NR, 2, PIECE, SHARE), vm(4, NR, 2, PIECE, SHARE),
            vm(NZ, NR, 2, PIECE, SHARE), vm(NZ, NR, PIECE, SHARE),
            dma(16), dma(11), dma(11),
            dma(2), dma(2), dma(2), dma(6), dma(6), dma(8), dma(8),
            dma(2 * NC), dma(2 * NC), dma(2 * NC), dma(6 * NC), dma(6 * NC), dma(8 * NC),
            dma(8 * NC),
            dma(NC), dma(NC), dma(6 * NC), dma(6 * NC), dma(2 * NC), dma(2 * NC), dma(NC), dma(NC),
            dma(1), dma(1), dma(16), dma(16), dma(8), dma(8), dma(8), dma(8),
            dma(8), dma(8), dma(8), dma(8), dma(16), dma(16),
        ],
        compiler_params=pltpu.CompilerParams(
            collective_id=0, has_side_effects=True, vmem_limit_bytes=60 * 2**20
        ),
    )(tokens, expert_ids.T, gate_probs.T, placement, jnp.swapaxes(gate_weight, 1, 2),
      jnp.swapaxes(up_weight, 1, 2), down_weight, out_grad, moment_first, moment_second)
    return outs


def solution(mesh):
    return jax.shard_map(
        step,
        mesh=mesh,
        in_specs=(
            P(("grp", "ep"), None),
            P(("grp", "ep"), None),
            P(("grp", "ep"), None),
            P("grp", None),
            P("grp", None, "ep"),
            P("grp", None, "ep"),
            P("grp", "ep", None),
            P(("grp", "ep"), None),
            P(None, "ep", "grp"),
            P(None, "ep", "grp"),
        ),
        out_specs=(
            P(("grp", "ep"), None),
            P("grp", "ep", None),
            P(None, "ep", "grp"),
            P(None, "ep", "grp"),
        ),
        check_vma=False,
    )
```

time: 110 us -> 103 us (0.936)
  Pallas kernels: 106 us -> 98.9 us
    pallas_call x1, Pallas kernels: 106 us -> 98.9 us  [step(): pl.pallas_call(body, out_shape=(vm(TOK, D), vm(1, HU, D), vm(2, HU, SHARE...]
where the time goes in v3:
time: 103 us
  Pallas kernels  98.9 us (96%)
  local copies, waits for them, and re-layouts  3.78 us (4%)
    pallas_call x1, Pallas kernels, step(): pl.pallas_call(body, out_shape=(vm(TOK, D), vm(1, HU, D), vm(2, HU, SHARE...  98.9 us
    unnamed x4, local copies, waits for them, and re-layouts  3.78 us

profile of v3, /device:TPU:8, one launch (start us, length us, event | category | flops | bytes accessed | tf_op | source)
XLA Modules:
  0.0 103.3 jit_solution(5243830856770923701)
XLA Ops:
  0.6 98.9 %shard_map.129 = (bf16[192,4096]{1,0:T(8,128)(2,1)S(1)}, bf16[1,192,4096]{2,1,0:T(8,128)(2,1)S(1)}, f32[2,192,256]{2,1,0:T(8,128)S(1)}, f32[2,192,256]{2,1,0:T(8,128)S(1)}) custom-call(bf16[192,4096]{1,0:T(8,128)(2,1)} %tok.1, s32[8,192]{1,0:T(8,128)} %bitcast.6, f32[8,192]{1,0:T(8,128)} %bitcast.7, s32[1,4]{1,0:T(1,128)} %plc.1, ...), custom_call_target="tpu_custom_call" | custom-call | tf_op jit(solution)/shard_map/pallas_call | solution.py:542
  99.5 1.1 %copy.18 = bf16[192,4096]{1,0:T(8,128)(2,1)} copy(bf16[192,4096]{1,0:T(8,128)(2,1)S(1)} %get-tuple-element.4) | data formatting | bytes 3145728
  100.7 0.7 copy.20
  101.4 0.7 copy.21
  102.1 1.1 %copy.19 = bf16[1,192,4096]{2,1,0:T(8,128)(2,1)} copy(bf16[1,192,4096]{2,1,0:T(8,128)(2,1)S(1)} %get-tuple-element.5) | data formatting | bytes 3145728

commit v4 on v3

--- a/solution.py
+++ b/solution.py
@@ -33,6 +33,8 @@
 
 XD = (2, 1, 3)
 NC = 4
+NTC = 2
+TCH = HALF // NTC
 NR = 2
 PIECE = HU // NR
 CHUNKS = ((4, 0), (3, 5), (2, 6), (1, 7))
@@ -80,12 +82,16 @@
         return pl.ds(pl.multiple_of(i * SHARE, SHARE), SHARE)
 
     mine_cols = pl.ds(pl.multiple_of(k * HALF, HALF), HALF)
-    other_cols = pl.ds(pl.multiple_of((1 - k) * HALF, HALF), HALF)
+
+    def tok_cols(core, c):
+        return pl.ds(pl.multiple_of(core * HALF + c * TCH, TCH), TCH)
 
     local = [
         pltpu.make_async_copy(ids, idsH.at[k], lsem.at[0]),
         pltpu.make_async_copy(prb, prbH.at[k], lsem.at[1]),
-        pltpu.make_async_copy(tok.at[:, mine_cols], tokH.at[k], lsem.at[2]),
+    ] + [
+        pltpu.make_async_copy(tok.at[:, tok_cols(k, c)], tokH.at[k, c], lsem.at[16 + c])
+        for c in range(NTC)
     ]
     local_g = [
         pltpu.make_async_copy(og.at[:, cols(2 * i + k)], grdH.at[k, i], lsem.at[8 + i])
@@ -111,7 +117,9 @@
     swap = [
         remote(ids, idsH.at[k], s_in.at[0], r_in.at[0], sib),
         remote(prb, prbH.at[k], s_in.at[1], r_in.at[1], sib),
-        remote(tok.at[:, other_cols], tokH.at[k], s_in.at[2], r_in.at[2], sib),
+    ] + [
+        remote(tok.at[:, tok_cols(1 - k, c)], tokH.at[k, c], s_in.at[11 + c], r_in.at[11 + c], sib)
+        for c in range(NTC)
     ]
     swap_g = [
         remote(og.at[:, cols(2 * i + 1 - k)], grdH.at[k, i], s_in.at[3 + i], r_in.at[3 + i], sib)
@@ -226,10 +234,13 @@
             for cp in self.y + self.x_near + self.x_far:
                 cp.wait_send()
 
-    toks = Route(
-        lambda s: snd_t.at[s], lambda c: xt.at[k, c], lambda p: rel_t.at[p],
-        (tl, tys, tyr, txs, txr, tfs, tfr), 0,
-    )
+    def tok_route(n):
+        return Route(
+            lambda s: snd_t.at[n, s], lambda chip: xt.at[k, n, chip], lambda p: rel_t.at[n, p],
+            (tl, tys, tyr, txs, txr, tfs, tfr), n,
+        )
+
+    toks = [tok_route(n) for n in range(NTC)]
     owner = [lax.rem(z + n, NZ) for n in range(NZ)]
 
     def grad_route(n):
@@ -240,14 +251,15 @@
 
     grads = [grad_route(n) for n in range(NC)]
 
-    local[2].wait()
-    swap[2].wait()
-    for c in range(NC):
-        at = slice(c * CH, (c + 1) * CH)
-        got = select(tokH[0, :, at], tokH[1, :, at])
-        snd_t[:, :, at] = got.astype(BF16).reshape(SLOTS, PAIR, CH)
-    toks.start_y()
-    toks.start_near()
+    for n in range(NTC):
+        local[2 + n].wait()
+        swap[2 + n].wait()
+        for c in range(0, TCH, CH):
+            at = slice(c, c + CH)
+            got = select(tokH[0, n, :, at], tokH[1, n, :, at])
+            snd_t[n, :, :, at] = got.astype(BF16).reshape(SLOTS, PAIR, CH)
+        toks[n].start_y()
+        toks[n].start_near()
     for cp in local_g + swap_g:
         cp.wait()
     for c, pair in enumerate(CHUNKS):
@@ -258,7 +270,8 @@
     for r in grads:
         r.start_y()
     grads[0].start_near()
-    toks.start_far()
+    for r in toks:
+        r.start_far()
     grads[0].start_far()
     for n in range(1, NC):
         grads[n].start_near()
@@ -267,11 +280,13 @@
         cp.wait()
     cand_copy.wait()
 
-    toks.arrive()
+    for r in toks:
+        r.arrive()
     pre_gate = jnp.zeros((ROWS, HU), F32)
     pre_up = jnp.zeros((ROWS, HU), F32)
     for c in range(0, D, CH):
-        rows = xt[c // HALF, :, :, c % HALF : c % HALF + CH].reshape(ROWS, CH)
+        at = c % TCH
+        rows = xt[c // HALF, c % HALF // TCH, :, :, at : at + CH].reshape(ROWS, CH)
         pre_gate += lax.dot_general(rows, wgv[:, c : c + CH], NT, preferred_element_type=F32)
         pre_up += lax.dot_general(rows, wuv[:, c : c + CH], NT, preferred_element_type=F32)
     sig = jax.nn.sigmoid(pre_gate)
@@ -324,10 +339,10 @@
 
     def ring(ring_hops, snd, rcv, t, n, first):
         for r in range(NR):
-            if t == 0 and r != first:
+            if t == 0 and (r < NR // 2) != first:
                 continue
             values = term(n, r)
-            more = t > 1 or (t == 1 and r == first)
+            more = t > 1 or (t == 1 and (r < NR // 2) == first)
             if more:
                 ring_hops[t - 1][r].wait_recv()
             for c in (0, 1):
@@ -338,10 +353,10 @@
             ring_hops[t][r].start()
 
     def down(t):
-        ring(downs, rm_snd, rm_rcv, t, 4 + t, 0)
+        ring(downs, rm_snd, rm_rcv, t, 4 + t, True)
 
     def up(t):
-        ring(ups, rp_snd, rp_rcv, t, 4 - t, 1)
+        ring(ups, rp_snd, rp_rcv, t, 4 - t, False)
 
     def d_hidden(c):
         got = None
@@ -489,14 +504,14 @@
 
     for t in range(4):
         for r in range(NR):
-            if t < 3 or r == 0:
+            if t < 3 or r < NR // 2:
                 a_up[t][r].wait_recv()
-                if t < 2 or (t == 2 and r == 0):
+                if t < 2 or (t == 2 and r < NR // 2):
                     a_up[t + 1][r].start()
                 use(1 + t, below[t + 1], r)
-            if t < 3 or r == 1:
+            if t < 3 or r >= NR // 2:
                 a_dn[t][r].wait_recv()
-                if t < 2 or (t == 2 and r == 1):
+                if t < 2 or (t == 2 and r >= NR // 2):
                     a_dn[t + 1][r].start()
                 use(5 + t if t < 3 else 4, above[t + 1], r)
         if t == 0:
@@ -513,7 +528,7 @@
 
     for cp in tg_copies + d_copies:
         cp.wait()
-    for r in [toks] + grads:
+    for r in toks + grads:
         r.end()
     for cp in far_copies:
         cp.wait_send()
@@ -521,15 +536,25 @@
         for cp in sent:
             cp.wait_send()
     for t in range(4):
-        for c in (0, 1):
-            if t > 0 or c == 0:
-                downs[t][c].wait_send()
-            if t > 0 or c == 1:
-                ups[t][c].wait_send()
-            if t < 3 or c == 0:
-                a_up[t][c].wait_send()
-            if t < 3 or c == 1:
-                a_dn[t][c].wait_send()
+        for r in range(NR):
+            low = r < NR // 2
+            if t > 0 or low:
+                downs[t][r].wait_send()
+            if t > 0 or not low:
+                ups[t][r].wait_send()
+            if t < 3 or low:
+                a_up[t][r].wait_send()
+            if t < 3 or not low:
+                a_dn[t][r].wait_send()
+
+
+def store(*refs):
+    sems = refs[-1]
+    copies = [pltpu.make_async_copy(refs[i], refs[4 + i], sems.at[i]) for i in range(4)]
+    for cp in copies:
+        cp.start()
+    for cp in copies:
+        cp.wait()
 
 
 def step(tokens, expert_ids, gate_probs, placement, gate_weight, up_weight, down_weight,
@@ -547,12 +572,12 @@
         in_specs=[anywhere] * 3 + [pl.BlockSpec(memory_space=pltpu.SMEM)] + [anywhere] * 6,
         out_specs=(pl.BlockSpec(memory_space=pltpu.VMEM),) * 4,
         scratch_shapes=[
-            vm(2, TOK, HALF), vm(2, NZ, TOK, SHARE),
+            vm(2, NTC, TOK, TCH), vm(2, NZ, TOK, SHARE),
             vm(2, 8, TOK, dtype=jnp.int32), vm(2, 8, TOK, dtype=F32),
             vm(2, TOK, SLOTS * PAIR),
-            vm(SLOTS, PAIR, HALF), vm(NC, SLOTS, PAIR, CH),
-            vm(2, PAIR, HALF), vm(NC, 2, PAIR, CH),
-            vm(2, CHIPS, PAIR, HALF), vm(2, NC, CHIPS, PAIR, CH),
+            vm(NTC, SLOTS, PAIR, TCH), vm(NC, SLOTS, PAIR, CH),
+            vm(NTC, 2, PAIR, TCH), vm(NC, 2, PAIR, CH),
+            vm(2, NTC, CHIPS, PAIR, TCH), vm(2, NC, CHIPS, PAIR, CH),
             vm(HU, D), vm(HU, D), vm(HU, D),
             vm(2, HU, SHARE, dtype=F32), vm(2, HU, SHARE, dtype=F32),
             vm(HU, ROWS), vm(ROWS, HU, dtype=F32), vm(ROWS, HU), vm(ROWS, HU),
@@ -565,20 +590,29 @@
             vm(4, NR, 2, PIECE, SHARE), vm(4, NR, 2, PIECE, SHARE),
             vm(4, NR, 2, PIECE, SHARE), vm(4, NR, 2, PIECE, SHARE),
             vm(NZ, NR, 2, PIECE, SHARE), vm(NZ, NR, PIECE, SHARE),
-            dma(16), dma(11), dma(11),
-            dma(2), dma(2), dma(2), dma(6), dma(6), dma(8), dma(8),
+            dma(16 + NTC), dma(11 + NTC), dma(11 + NTC),
+            dma(2 * NTC), dma(2 * NTC), dma(2 * NTC), dma(6 * NTC), dma(6 * NTC), dma(8 * NTC),
+            dma(8 * NTC),
             dma(2 * NC), dma(2 * NC), dma(2 * NC), dma(6 * NC), dma(6 * NC), dma(8 * NC),
             dma(8 * NC),
             dma(NC), dma(NC), dma(6 * NC), dma(6 * NC), dma(2 * NC), dma(2 * NC), dma(NC), dma(NC),
-            dma(1), dma(1), dma(16), dma(16), dma(8), dma(8), dma(8), dma(8),
-            dma(8), dma(8), dma(8), dma(8), dma(16), dma(16),
+            dma(1), dma(1), dma(NZ * NR), dma(NZ * NR),
+            dma(4 * NR), dma(4 * NR), dma(4 * NR), dma(4 * NR),
+            dma(4 * NR), dma(4 * NR), dma(4 * NR), dma(4 * NR), dma(NZ * NR), dma(NZ * NR),
         ],
         compiler_params=pltpu.CompilerParams(
             collective_id=0, has_side_effects=True, vmem_limit_bytes=60 * 2**20
         ),
     )(tokens, expert_ids.T, gate_probs.T, placement, jnp.swapaxes(gate_weight, 1, 2),
       jnp.swapaxes(up_weight, 1, 2), down_weight, out_grad, moment_first, moment_second)
-    return outs
+    return pl.pallas_call(
+        store,
+        out_shape=tuple(jax.ShapeDtypeStruct(o.shape, o.dtype) for o in outs),
+        in_specs=[pl.BlockSpec(memory_space=pltpu.VMEM)] * 4,
+        out_specs=(anywhere,) * 4,
+        scratch_shapes=[dma(4)],
+        compiler_params=pltpu.CompilerParams(vmem_limit_bytes=2**20),
+    )(*[pltpu.with_memory_space_constraint(o, pltpu.VMEM) for o in outs])
 
 
 def solution(mesh):

time: 103 us -> 100 us (0.971)
  local copies, waits for them, and re-layouts: 3.78 us -> 0 us
    unnamed x4 -> x0, local copies, waits for them, and re-layouts: 3.78 us -> none
    pallas_call x0 -> x1, Pallas kernels: none -> 1.95 us  [step(): pl.pallas_call(store, out_shape=tuple((jax.ShapeDtypeStruct(o.shape, o.dt...]
    pallas_call x1, Pallas kernels: 98.9 us -> 97.6 us  [step(): pl.pallas_call(body, out_shape=(vm(TOK, D), vm(1, HU, D), vm(2, HU, SHARE...]
where the time goes in v4:
time: 100 us
  Pallas kernels  99.6 us (100%)
    pallas_call x1, Pallas kernels, step(): pl.pallas_call(body, out_shape=(vm(TOK, D), vm(1, HU, D), vm(2, HU, SHARE...  97.6 us

profile of v4, /device:TPU:8, one launch (start us, length us, event | category | flops | bytes accessed | tf_op | source)
XLA Modules:
  0.0 100.2 jit_solution(18170026987984544967)
XLA Ops:
  0.6 97.6 %shard_map.129 = (bf16[192,4096]{1,0:T(8,128)(2,1)S(1)}, bf16[1,192,4096]{2,1,0:T(8,128)(2,1)S(1)}, f32[2,192,256]{2,1,0:T(8,128)S(1)}, f32[2,192,256]{2,1,0:T(8,128)S(1)}) custom-call(bf16[192,4096]{1,0:T(8,128)(2,1)} %tok.1, s32[8,192]{1,0:T(8,128)} %bitcast.6, f32[8,192]{1,0:T(8,128)} %bitcast.7, s32[1,4]{1,0:T(1,128)} %plc.1, ...), custom_call_target="tpu_custom_call" | custom-call | tf_op jit(solution)/shard_map/pallas_call | solution.py:567
  98.3 1.9 %shard_map.130 = (bf16[192,4096]{1,0:T(8,128)(2,1)}, bf16[1,192,4096]{2,1,0:T(8,128)(2,1)}, f32[2,192,256]{2,1,0:T(8,128)}, f32[2,192,256]{2,1,0:T(8,128)}) custom-call(bf16[192,4096]{1,0:T(8,128)(2,1)S(1)} %get-tuple-element.8.refs_0_, bf16[1,192,4096]{2,1,0:T(8,128)(2,1)S(1)} %get-tuple-element.9.refs_1_, f32[2,192,256]{2,1,0:T(8,128)S(1)} %get-tuple-element.10.refs_2_, ...), custom_call_target="tpu_custom_call" | custom-call | tf_op jit(solution)/shard_map/pallas_call | solution.py:608

commit v5 on v4

--- a/solution.py
+++ b/solution.py
@@ -385,12 +385,12 @@
     d_hidden(2)
     grads[3].arrive()
     shares(CHUNKS[3])
+    up(2)
+    down(2)
     d_hidden(3)
     d_hid = dhv[...]
     dgv[...] = (d_hid * pre_up * sig * (1.0 + pre_gate * (1.0 - sig))).astype(BF16)
     duv[...] = (d_hid * act).astype(BF16)
-    up(2)
-    down(2)
 
     def partial(start):
         at = pl.ds(pl.multiple_of(start, CH), CH)
@@ -404,6 +404,8 @@
         got = partial((1 - k) * HALF + c * CH)
         p_snd[c] = got.astype(BF16).reshape(CHIPS, PAIR, CH)
         p_copies[c].start()
+    up(3)
+    down(3)
     for c in range(NC):
         p_own[c] = partial(k * HALF + c * CH).reshape(CHIPS, PAIR, CH)
 
@@ -427,8 +429,6 @@
         fin[c, x] = both_cores(q)
         r_copies.append(sent)
 
-    up(3)
-    down(3)
     for c in range(NC):
         send_back(c)
 

time: 100 us -> 100 us (level)
  no operation moved by 1% of the time
where the time goes in v5:
time: 100 us
  Pallas kernels  99.4 us (99%)
    pallas_call x1, Pallas kernels, step(): pl.pallas_call(body, out_shape=(vm(TOK, D), vm(1, HU, D), vm(2, HU, SHARE...  97.5 us

profile of v5, /device:TPU:8, one launch (start us, length us, event | category | flops | bytes accessed | tf_op | source)
XLA Modules:
  0.0 100.1 jit_solution(9081666293466033047)
XLA Ops:
  0.6 97.5 %shard_map.129 = (bf16[192,4096]{1,0:T(8,128)(2,1)S(1)}, bf16[1,192,4096]{2,1,0:T(8,128)(2,1)S(1)}, f32[2,192,256]{2,1,0:T(8,128)S(1)}, f32[2,192,256]{2,1,0:T(8,128)S(1)}) custom-call(bf16[192,4096]{1,0:T(8,128)(2,1)} %tok.1, s32[8,192]{1,0:T(8,128)} %bitcast.6, f32[8,192]{1,0:T(8,128)} %bitcast.7, s32[1,4]{1,0:T(1,128)} %plc.1, ...), custom_call_target="tpu_custom_call" | custom-call | tf_op jit(solution)/shard_map/pallas_call | solution.py:567
  98.1 1.9 %shard_map.130 = (bf16[192,4096]{1,0:T(8,128)(2,1)}, bf16[1,192,4096]{2,1,0:T(8,128)(2,1)}, f32[2,192,256]{2,1,0:T(8,128)}, f32[2,192,256]{2,1,0:T(8,128)}) custom-call(bf16[192,4096]{1,0:T(8,128)(2,1)S(1)} %get-tuple-element.8.refs_0_, bf16[1,192,4096]{2,1,0:T(8,128)(2,1)S(1)} %get-tuple-element.9.refs_1_, f32[2,192,256]{2,1,0:T(8,128)S(1)} %get-tuple-element.10.refs_2_, ...), custom_call_target="tpu_custom_call" | custom-call | tf_op jit(solution)/shard_map/pallas_call | solution.py:608
